TPU v7x, 32 devices: a whole 2x2x4 slice. The times are simulated.
32 devices in a mesh: fsdp: 16 (over z, y, x), replica: 2 (over core).
Axes of the slice: x: 2, y: 2, z: 4, core: 2. Of those that a mesh axis runs over, the one named last changes fastest.
Arguments:
- tokens: bfloat16 [4352, 1024], P(('fsdp', 'replica')), may hold values from -6 to 6
- cotangent: bfloat16 [4352, 1024], P(('fsdp', 'replica')), may hold values from -6 to 6
- w_in: bfloat16 [1024, 3072], P('fsdp'), may hold values from -0.1875 to 0.1875
- w_out: bfloat16 [1024, 1024], P('fsdp'), may hold values from -0.1875 to 0.1875
- w_gate: bfloat16 [1024, 4608], P('fsdp'), may hold values from -0.1875 to 0.1875
- w_up: bfloat16 [1024, 4608], P('fsdp'), may hold values from -0.1875 to 0.1875
- w_down: bfloat16 [4608, 1024], P('fsdp'), may hold values from -0.09375 to 0.09375
- norm1_scale: float32 [1024], replicated, may hold values from 0.5 to 1.5
- norm2_scale: float32 [1024], replicated, may hold values from 0.5 to 1.5
- conv_weight: float32 [3, 1024], replicated, may hold values from -3 to 3
- dev_extra: int32 [32], replicated, may hold values from 1 to 134, 4032 in all
- seq_lengths: int32 [6], replicated, may hold values from 1 to 1024, 4096 in all
Outputs:
- block_out: bfloat16 [4352, 1024], P(('fsdp', 'replica'))
- d_tokens: bfloat16 [4352, 1024], P(('fsdp', 'replica'))
- d_w_in: float32 [1024, 3072], P('fsdp')
- d_w_out: float32 [1024, 1024], P('fsdp')
- d_w_gate: float32 [1024, 4608], P('fsdp')
- d_w_up: float32 [1024, 4608], P('fsdp')
- d_w_down: float32 [4608, 1024], P('fsdp')
- d_norm1: float32 [1024], replicated
- d_norm2: float32 [1024], replicated
- d_conv: float32 [3, 1024], replicated
Inputs may be any that keep to these rules, and one draw needn't show every extreme that they name: Device d holds dev_extra[d] + 2 consecutive packed tokens in its first rows, devices in the order of fsdp+replica, the rest of its 136 rows are padding; some device is full in every draw. `seq_lengths`: the sequences are packed back to back in this order over all tokens, one of them exactly 1024 long.
All inputs are finite; a program needn't handle non-finite values.
Results may differ from a plain program's by a relative error of at most 0.011.
Values may be sent and summed in bfloat16 or wider, within the bound.
A program may use at most 320 MiB of HBM per device.

v0:
```python
import jax
import jax.numpy as jnp
from jax import lax
from jax.sharding import PartitionSpec as P

epsilon = 1e-05


def passed_along(block, axis, distance):
    devices = range(lax.axis_size(axis))
    route = [(i - distance, i) for i in devices if i - distance in devices]
    return lax.ppermute(block, axis, route)


def rms_scale(v):
    return lax.rsqrt(jnp.mean(v * v, axis=-1, keepdims=True) + epsilon)


def product(left, right):
    return jnp.dot(left, right, preferred_element_type=jnp.float32)


def product_left(left, right):
    return lax.dot_general(
        left, right, (((0,), (0,)), ((), ())), preferred_element_type=jnp.float32
    )


def product_right(left, right):
    return lax.dot_general(
        left, right, (((1,), (1,)), ((), ())), preferred_element_type=jnp.float32
    )


def norm_back(grad, scaled, scale, gain):
    grad_gain = grad * gain
    return scale * (grad_gain - scaled * jnp.mean(grad_gain * scaled, axis=-1, keepdims=True))


def body(
    tokens,
    cotangent,
    w_in,
    w_out,
    w_gate,
    w_up,
    w_down,
    norm1_scale,
    norm2_scale,
    conv_weight,
    dev_extra,
    seq_lengths,
):
    shards = (w_in, w_out, w_gate, w_up, w_down)
    whole_in, whole_out, whole_gate, whole_up, whole_down = (
        lax.all_gather(shards[0], "fsdp", axis=0, tiled=True),
        lax.all_gather(shards[1], "fsdp", axis=0, tiled=True),
        lax.all_gather(shards[2], "fsdp", axis=0, tiled=True),
        lax.all_gather(shards[3], "fsdp", axis=0, tiled=True),
        lax.all_gather(shards[4], "fsdp", axis=0, tiled=True),
    )
    rows_dev = tokens.shape[0]
    width = tokens.shape[1]
    hidden = whole_down.shape[0]
    device = lax.axis_index(("fsdp", "replica"))
    counts = dev_extra + 2
    end_rows = jnp.cumsum(counts)
    device_ids = jnp.arange(counts.shape[0], dtype=jnp.int32)
    mine = device_ids == device
    count = jnp.sum(jnp.where(mine, counts, 0))
    offset = jnp.sum(jnp.where(mine, end_rows, 0)) - count
    row_ids = jnp.arange(rows_dev, dtype=jnp.int32)
    valid = row_ids < count
    position = offset + row_ids
    seq_first = jnp.cumsum(seq_lengths) - seq_lengths
    is_start = jnp.any(position[:, None] == seq_first[None, :], axis=1)
    prev_start = jnp.any((position - 1)[:, None] == seq_first[None, :], axis=1)
    keep_one = (valid & jnp.logical_not(is_start)).astype(jnp.float32)[:, None]
    keep_two = keep_one * jnp.logical_not(prev_start).astype(jnp.float32)[:, None]
    inputs = tokens.astype(jnp.float32)
    scale_one = rms_scale(inputs)
    scaled_one = inputs * scale_one
    normed_in = (scaled_one * norm1_scale).astype(jnp.bfloat16)
    in_proj = product(normed_in, whole_in).astype(jnp.bfloat16)
    b_part = in_proj[:, :width]
    c_part = in_proj[:, width : 2 * width]
    x_part = in_proj[:, 2 * width :]
    rim_pair = (
        lax.dynamic_slice_in_dim(b_part, count - 2, 2, 0),
        lax.dynamic_slice_in_dim(x_part, count - 2, 2, 0),
    )
    rim_b, rim_x = passed_along((rim_pair[0], rim_pair[1]), ("fsdp", "replica"), 1)
    b_val = b_part.astype(jnp.float32)
    x_val = x_part.astype(jnp.float32)
    c_val = c_part.astype(jnp.float32)
    u = b_val * x_val
    u_ext = jnp.concatenate([rim_b.astype(jnp.float32) * rim_x.astype(jnp.float32), u], axis=0)
    u_prev = u_ext[1 : rows_dev + 1] * keep_one
    u_prev2 = u_ext[:rows_dev] * keep_two
    v = conv_weight[2] * u + conv_weight[1] * u_prev + conv_weight[0] * u_prev2
    y_val = (c_val * v).astype(jnp.bfloat16)
    hidden_res = inputs + product(y_val, whole_out)
    scale_two = rms_scale(hidden_res)
    scaled_two = hidden_res * scale_two
    normed_ffn = (scaled_two * norm2_scale).astype(jnp.bfloat16)
    gate_val = product(normed_ffn, whole_gate)
    up_val = product(normed_ffn, whole_up)
    sigma = jax.nn.sigmoid(gate_val)
    silu_val = gate_val * sigma
    act_val = (silu_val * up_val).astype(jnp.bfloat16)
    result = hidden_res + product(act_val, whole_down)
    block_out = jnp.where(valid[:, None], result, 0.0).astype(jnp.bfloat16)
    grad_out = jnp.where(valid[:, None], cotangent, jnp.zeros_like(cotangent))
    grad_act = product_right(grad_out, whole_down)
    grad_gate = (grad_act * up_val * sigma * (1.0 + gate_val * (1.0 - sigma))).astype(jnp.bfloat16)
    grad_up = (grad_act * silu_val).astype(jnp.bfloat16)
    grad_ffn = product_right(grad_gate, whole_gate) + product_right(grad_up, whole_up)
    gain_two = jnp.sum(grad_ffn * scaled_two, axis=0)
    grad_res = grad_out.astype(jnp.float32) + norm_back(
        grad_ffn, scaled_two, scale_two, norm2_scale
    )
    grad_mix = grad_res.astype(jnp.bfloat16)
    grad_y = product_right(grad_mix, whole_out)
    grad_c = grad_y * v
    grad_v = grad_y * c_val
    conv_grads = jnp.stack(
        [
            jnp.sum(grad_v * u_prev2, axis=0),
            jnp.sum(grad_v * u_prev, axis=0),
            jnp.sum(grad_v * u, axis=0),
        ]
    )
    term_one = conv_weight[1] * keep_one * grad_v
    term_two = conv_weight[0] * keep_two * grad_v
    grad_ext = (
        jnp.pad(term_two, ((0, 2), (0, 0)))
        + jnp.pad(term_one, ((1, 1), (0, 0)))
        + jnp.pad(conv_weight[2] * grad_v, ((2, 0), (0, 0)))
    )
    from_next = passed_along(grad_ext[:2], ("fsdp", "replica"), -1)
    grad_u = grad_ext[2:]
    grad_u = grad_u + lax.dynamic_update_slice_in_dim(
        jnp.zeros_like(grad_u), from_next, count - 2, 0
    )
    grad_proj = jnp.concatenate([grad_u * x_val, grad_c, grad_u * b_val], axis=1).astype(
        jnp.bfloat16
    )
    grad_norm_in = product_right(grad_proj, whole_in)
    gain_one = jnp.sum(grad_norm_in * scaled_one, axis=0)
    d_tokens = (grad_res + norm_back(grad_norm_in, scaled_one, scale_one, norm1_scale)).astype(
        jnp.bfloat16
    )
    d_norm1, d_norm2, d_conv = lax.psum((gain_one, gain_two, conv_grads), ("fsdp", "replica"))
    grad_pair = jnp.concatenate([grad_gate, grad_up], axis=1)
    pieces = [
        product_left(left, right)
        for left, right in ((normed_in, grad_proj), (y_val, grad_mix), (normed_ffn, grad_pair))
    ]
    rows_part = lax.psum_scatter(
        jnp.concatenate(pieces, axis=1), "fsdp", scatter_dimension=0, tiled=True
    )
    down_part = lax.psum_scatter(
        product_left(act_val, grad_out), "fsdp", scatter_dimension=0, tiled=True
    )
    rows_part, down_part = (
        lax.psum(rows_part.astype(jnp.bfloat16), "replica").astype(jnp.float32),
        lax.psum(down_part.astype(jnp.bfloat16), "replica").astype(jnp.float32),
    )
    d_w_in = rows_part[:, : 3 * width]
    d_w_out = rows_part[:, 3 * width : 4 * width]
    d_w_gate = rows_part[:, 4 * width : 4 * width + hidden]
    d_w_up = rows_part[:, 4 * width + hidden :]
    return (
        block_out,
        d_tokens,
        d_w_in,
        d_w_out,
        d_w_gate,
        d_w_up,
        down_part,
        d_norm1,
        d_norm2,
        d_conv,
    )


def solution(mesh):
    placed = (
        P(("fsdp", "replica"), None),
        P(("fsdp", "replica"), None),
        P("fsdp", None),
        P("fsdp", None),
        P("fsdp", None),
        P("fsdp", None),
        P("fsdp", None),
        P(),
        P(),
        P(),
        P(),
        P(),
    )
    return jax.shard_map(
        body,
        mesh=mesh,
        in_specs=placed,
        out_specs=(
            P(("fsdp", "replica"), None),
            P(("fsdp", "replica"), None),
            P("fsdp", None),
            P("fsdp", None),
            P("fsdp", None),
            P("fsdp", None),
            P("fsdp", None),
            P(),
            P(),
            P(),
        ),
        check_vma=False,
    )
```

profile of v0, /device:TPU:0, one launch (start us, length us, event | category | flops | bytes accessed | tf_op | source)
XLA Modules:
  0.0 2023.8 jit_solution(4357965801380249260)
XLA Ops:
  7.3 0.7 all-gather.6.cloned.1.call-update
  8.0 0.7 all-gather.8.cloned.1.call-update
  8.7 0.7 all-gather.12.cloned.1.call-update
  9.5 0.5 all-gather.10.cloned.1.call-update
  10.0 0.5 all-gather.14.cloned.1.call-update
  10.6 0.0 reduce-scatter.5.cloned.1.call-start
  10.6 1.3 add_bitcast_fusion
  13.2 0.8 reduce-window.19
  14.1 0.1 copy.26
  14.2 0.1 reduce-window.18
  14.2 0.1 reduce
  14.3 0.6 fusion.34
  16.3 0.7 iota_compare_fusion
  16.9 0.7 bitcast_subtract_fusion
  17.6 0.1 compare_reduce_fusion.1
  17.7 0.1 fusion.23
  17.8 0.7 and_convert_fusion
  18.5 0.7 broadcast_select_fusion.1
  19.2 88.5 %all-gather.6.cloned.1.call-done = bf16[1024,3072]{1,0:T(8,128)(2,1)} async-done(((bf16[64,3072]{1,0:T(8,128)(2,1)}), bf16[1024,3072]{1,0:T(8,128)(2,1)}) %all-gather.6.cloned.1.call-update) | async-done | bytes 6291472 | tf_op jit(solution)/shard_map/all_gather | solution.py:56
  107.7 3.9 convolution_convert_fusion
  111.7 1.3 collective-permute-start.1
  113.0 4.1 collective-permute-start
  117.1 0.1 convert_multiply_fusion.3
  117.2 0.7 collective-permute-done
  117.9 0.3 multiply_add_fusion.1
  118.2 51.3 %all-gather.8.cloned.1.call-done = bf16[1024,1024]{1,0:T(8,128)(2,1)} async-done(((bf16[64,1024]{1,0:T(8,128)(2,1)}), bf16[1024,1024]{1,0:T(8,128)(2,1)}) %all-gather.8.cloned.1.call-update) | async-done | bytes 2097168 | tf_op jit(solution)/shard_map/all_gather | solution.py:57
  169.5 2.2 multiply_reduce_fusion.5
  171.7 0.1 multiply_convert_fusion.4
  171.8 121.6 %all-gather.12.cloned.1.call-done = bf16[1024,4608]{1,0:T(8,128)(2,1)} async-done(((bf16[64,4608]{1,0:T(8,128)(2,1)}), bf16[1024,4608]{1,0:T(8,128)(2,1)}) %all-gather.12.cloned.1.call-update) | async-done | bytes 9437200 | tf_op jit(solution)/shard_map/all_gather | solution.py:59
  293.4 6.6 fusion.46
  300.0 116.7 %all-gather.10.cloned.1.call-done = bf16[1024,4608]{1,0:T(8,128)(2,1)} async-done(((bf16[64,4608]{1,0:T(8,128)(2,1)}), bf16[1024,4608]{1,0:T(8,128)(2,1)}) %all-gather.10.cloned.1.call-update) | async-done | bytes 9437200 | tf_op jit(solution)/shard_map/all_gather | solution.py:58
  416.7 6.6 fusion.45
  423.3 116.7 %all-gather.14.cloned.1.call-done = bf16[4608,1024]{1,0:T(8,128)(2,1)} async-done(((bf16[288,1024]{1,0:T(8,128)(2,1)}), bf16[4608,1024]{1,0:T(8,128)(2,1)}) %all-gather.14.cloned.1.call-update) | async-done | bytes 9437200 | tf_op jit(solution)/shard_map/all_gather | solution.py:60
  540.1 10.3 multiply_convert_fusion
  550.4 8.0 fusion.38
  558.4 0.2 reduce-scatter.3.cloned.1.call-start
  558.6 1.0 copy-done.8
  559.7 6.9 fusion.47
  566.7 7.1 multiply_reduce_fusion.3
  573.8 0.2 multiply_add_fusion
  574.1 1.7 multiply_reduce_fusion.2
  575.8 0.2 multiply_multiply_fusion.1
  576.0 1.4 collective-permute-start.2
  577.5 2.8 fusion.27
  580.3 15.8 fusion
  596.0 0.2 pad_add_fusion
  596.3 0.2 add.126
  596.5 0.1 fusion.15
  596.7 0.5 copy-done.16
  597.2 6.4 fusion.25
  603.6 37.3 %pad_maximum_fusion = f32[1024,13312]{1,0:T(8,128)} fusion(f32[1024,9216]{1,0:T(8,128)} %fusion, f32[1024,1024]{1,0:T(8,128)} %fusion.27, f32[1024,3072]{1,0:T(8,128)} %fusion.25), kind=kLoop, calls=%fused_computation | loop fusion | flops 27262976 | bytes 109051904 | tf_op jit(solution)/shard_map/concatenate | solution.py:160
  640.9 0.3 all-reduce.7.cloned.1.call-start
  641.1 200.9 %reduce-scatter.5.cloned.1.call-done = f32[288,1024]{1,0:T(8,128)} async-done(((f32[4608,1024]{1,0:T(8,128)}), f32[288,1024]{1,0:T(8,128)}) %reduce-scatter.5.cloned.1.call-update) | async-done | bytes 1179664 | tf_op jit(solution)/shard_map/reduce_scatter | solution.py:162
  842.0 2.2 convert_element_type.102
  844.2 1106.3 %reduce-scatter.3.cloned.1.call-done = f32[64,13312]{1,0:T(8,128)} async-done(((f32[1024,13312]{1,0:T(8,128)}), f32[64,13312]{1,0:T(8,128)}) %reduce-scatter.3.cloned.1.call-update) | async-done | bytes 3407888 | tf_op jit(solution)/shard_map/reduce_scatter | solution.py:159
  1950.5 3.5 convert_element_type.100
  1954.1 6.4 fusion.6
  1960.5 3.0 fusion.22
  1963.5 45.0 %all-reduce.3 = (f32[1024]{0:T(1024)}, f32[1024]{0:T(1024)}, f32[3,1024]{1,0:T(4,128)}) all-reduce(f32[1024]{0:T(1024)S(1)} %get-tuple-element.14, f32[1024]{0:T(1024)S(1)} %get-tuple-element.12, f32[3,1024]{1,0:T(4,128)S(1)} %pad_maximum_fusion.5), channel_id=1, replica_groups=mesh['fsdp'=16,'replica'=2] {'fsdp','replica'}, use_global_device_ids=true, to_apply=%region_15.16 | all-reduce | flops 5120 | bytes 40960 | tf_op jit(solution)/shard_map/psum | solution.py:153
  2008.6 2.0 fusion.21
  2010.5 1.8 slice.69
  2012.3 1.9 slice.68
  2014.2 1.6 fusion.42
  2015.9 1.1 convert_element_type.103
  (68 shorter events, 0.6 us)
Async XLA Ops:
  7.2 10.5 copy-start.1
  7.2 12.0 copy-start.19
  7.2 100.5 %copy-start.15 = (f32[1024]{0:T(1024)S(1)}, f32[1024]{0:T(1024)}, u32[]{:S(2)}) copy-start(f32[1024]{0:T(1024)} %param.19) | copy-start | bytes 12292
  7.2 100.5 %all-gather.6.cloned.1.call-start = ((), (), s32[]{:S(2)}) async-start(), calls=%async_computation.2 | async-start | bytes 6684672 | tf_op jit(solution)/shard_map/all_gather | solution.py:56
  7.9 161.5 %all-gather.8.cloned.1.call-start = ((), (), s32[]{:S(2)}) async-start(), calls=%async_computation.3 | async-start | bytes 2228224 | tf_op jit(solution)/shard_map/all_gather | solution.py:57
  8.7 284.7 %all-gather.12.cloned.1.call-start = ((), (), s32[]{:S(2)}) async-start(), calls=%async_computation.5 | async-start | bytes 10027008 | tf_op jit(solution)/shard_map/all_gather | solution.py:59
  9.4 407.3 %all-gather.10.cloned.1.call-start = ((), (), s32[]{:S(2)}) async-start(), calls=%async_computation.4 | async-start | bytes 10027008 | tf_op jit(solution)/shard_map/all_gather | solution.py:58
  10.0 530.1 %all-gather.14.cloned.1.call-start = ((), (), s32[]{:S(2)}) async-start(), calls=%async_computation.6 | async-start | bytes 10027008 | tf_op jit(solution)/shard_map/all_gather | solution.py:60
  10.6 831.4 %reduce-scatter.5.cloned.1.call-start = ((), (), s32[]{:S(2)}) async-start(), calls=%async_computation.8 | async-start | bytes 20054016 | tf_op jit(solution)/shard_map/reduce_scatter | solution.py:162
  111.7 5.5 collective-permute-start.1
  113.0 4.9 collective-permute-start
  117.2 54.6 %copy-start.10 = (f32[136,1024]{1,0:T(8,128)}, f32[136,1024]{1,0:T(8,128)S(1)}, u32[]{:S(2)}) copy-start(f32[136,1024]{1,0:T(8,128)S(1)} %convert_multiply_fusion.3) | copy-start | bytes 1671172
  117.2 54.5 %copy-start.18 = (f32[1024]{0:T(1024)S(1)}, f32[1024]{0:T(1024)}, u32[]{:S(2)}) copy-start(f32[1024]{0:T(1024)} %param.20) | copy-start | bytes 12292
  118.2 181.8 %copy-start.5 = (f32[136,1024]{1,0:T(8,128)}, f32[136,1024]{1,0:T(8,128)S(1)}, u32[]{:S(2)}) copy-start(f32[136,1024]{1,0:T(8,128)S(1)} %multiply_add_fusion.1) | copy-start | bytes 1671172
  300.0 240.1 %copy-start.13 = (bf16[136,1024]{1,0:T(8,128)(2,1)S(1)}, bf16[136,1024]{1,0:T(8,128)(2,1)}, u32[]{:S(2)}) copy-start(bf16[136,1024]{1,0:T(8,128)(2,1)} %param.13) | copy-start | bytes 835588
  550.4 8.0 copy-start
  558.4 1.3 copy-start.8
  558.4 1392.1 %reduce-scatter.3.cloned.1.call-start = ((), (), s32[]{:S(2)}) async-start(), calls=%async_computation.7 | async-start | bytes 57933824 | tf_op jit(solution)/shard_map/reduce_scatter | solution.py:159
  559.7 7.0 copy-start.7
  566.6 7.4 copy-start.6
  566.6 7.4 copy-start.11
  566.7 7.4 copy-start.12
  574.1 3.4 copy-start.3
  576.0 4.3 copy-start.9
  576.0 20.3 %collective-permute-start.2 = (f32[2,1024]{1,0:T(2,128)S(1)}, f32[2,1024]{1,0:T(2,128)S(1)}, u32[]{:S(2)}, u32[]{:S(2)}) collective-permute-start(f32[2,1024]{1,0:T(2,128)S(1)} %pad_add_fusion.1), channel_id=1, source_target_pairs={{1,0},{2,1},{3,2},{4,3},{5,4},{6,5},{7,6},{8,7},{9,8},{10,9},{11,1... | collective-permute-start | bytes 24584 | tf_op jit(solution)/shard_map/ppermute | solution.py:12
  596.2 1.0 copy-start.16
  640.9 1369.7 %all-reduce.7.cloned.1.call-start = ((), (), s32[]{:S(2)}) async-start(), calls=%async_computation.9 | async-start | bytes 4587520 | tf_op jit(solution)/shard_map/psum | solution.py:166
  1950.5 9.9 slice-start
  1954.0 6.4 slice-start.1
  1954.0 6.4 copy-start.17
  1960.5 48.1 %copy-start.4 = (f32[136,1024]{1,0:T(8,128)S(1)}, f32[136,1024]{1,0:T(8,128)}, u32[]{:S(2)}) copy-start(f32[136,1024]{1,0:T(8,128)} %copy-done.3) | copy-start | bytes 1671172
  2010.5 3.7 copy-start.2
  2014.2 1.6 copy-start.14
Sparse Core Ops, SparseCore 0:
  10.8 96.8 all-gather.5
  110.5 58.9 all-gather.7
  172.3 121.0 all-gather.11
  296.1 120.6 all-gather.9
  419.4 120.6 all-gather.13
  558.5 283.4 reduce-scatter.4
  844.4 1106.0 reduce-scatter.2
  1954.1 27.3 all-reduce.6
where the time goes:
time: 2020 us
  waiting for transfers between devices  1810 us (90%)
  matrix products  87.8 us (4%)
  other arithmetic  53 us (3%)
  blocking collectives  45 us (2%)
    reduce_scatter x1, waiting for transfers between devices, body(): lax.psum_scatter(jnp.concatenate(pieces, axis=1), 'fsdp', scatter_dimensi...  1110 us
    reduce_scatter x1, waiting for transfers between devices, body(): lax.psum_scatter(product_left(act_val, grad_out), 'fsdp', scatter_dimensi...  201 us
    all_gather x1, waiting for transfers between devices, body(): lax.all_gather(shards[3], 'fsdp', axis=0, tiled=True)  122 us
    all_gather x1, waiting for transfers between devices, body(): lax.all_gather(shards[4], 'fsdp', axis=0, tiled=True)  117 us
    all_gather x1, waiting for transfers between devices, body(): lax.all_gather(shards[2], 'fsdp', axis=0, tiled=True)  117 us
    all_gather x1, waiting for transfers between devices, body(): lax.all_gather(shards[0], 'fsdp', axis=0, tiled=True)  88.5 us
    all_gather x1, waiting for transfers between devices, body(): lax.all_gather(shards[1], 'fsdp', axis=0, tiled=True)  51.3 us
    psum x1, blocking collectives, body(): lax.psum((gain_one, gain_two, conv_grads), ('fsdp', 'replica'))  45 us
  transfers between devices with their start and end apart: 11, of which 8 were waited for; matrix products, arithmetic and copies ran while one was open for 6% of the time, Pallas kernels for 0%

commit v1 on v0

--- a/solution.py
+++ b/solution.py
@@ -30,6 +30,12 @@
     return lax.dot_general(
         left, right, (((1,), (1,)), ((), ())), preferred_element_type=jnp.float32
     )
+
+
+def scattered_sum(value):
+    return lax.psum_scatter(
+        value.astype(jnp.bfloat16), "fsdp", scatter_dimension=0, tiled=True
+    ).astype(jnp.float32)
 
 
 def norm_back(grad, scaled, scale, gain):
@@ -51,17 +57,20 @@
     dev_extra,
     seq_lengths,
 ):
-    shards = (w_in, w_out, w_gate, w_up, w_down)
-    whole_in, whole_out, whole_gate, whole_up, whole_down = (
-        lax.all_gather(shards[0], "fsdp", axis=0, tiled=True),
-        lax.all_gather(shards[1], "fsdp", axis=0, tiled=True),
-        lax.all_gather(shards[2], "fsdp", axis=0, tiled=True),
-        lax.all_gather(shards[3], "fsdp", axis=0, tiled=True),
-        lax.all_gather(shards[4], "fsdp", axis=0, tiled=True),
-    )
     rows_dev = tokens.shape[0]
     width = tokens.shape[1]
-    hidden = whole_down.shape[0]
+    hidden = w_gate.shape[1]
+    group = lax.axis_size("fsdp")
+    part = w_down.shape[0]
+    whole_in = lax.all_gather(w_in, "fsdp", axis=0, tiled=True)
+    whole_out = lax.all_gather(w_out, "fsdp", axis=0, tiled=True)
+    own_rows = w_gate.shape[0]
+    pair = jnp.concatenate(
+        [w_gate.reshape(own_rows, group, part), w_up.reshape(own_rows, group, part)], axis=2
+    )
+    pair = lax.all_to_all(
+        pair.transpose(1, 0, 2), "fsdp", split_axis=0, concat_axis=0, tiled=True
+    ).reshape(width, 2 * part)
     device = lax.axis_index(("fsdp", "replica"))
     counts = dev_extra + 2
     end_rows = jnp.cumsum(counts)
@@ -89,7 +98,8 @@
         lax.dynamic_slice_in_dim(b_part, count - 2, 2, 0),
         lax.dynamic_slice_in_dim(x_part, count - 2, 2, 0),
     )
-    rim_b, rim_x = passed_along((rim_pair[0], rim_pair[1]), ("fsdp", "replica"), 1)
+    rim = passed_along(jnp.concatenate(rim_pair, axis=0), ("fsdp", "replica"), 1)
+    rim_b, rim_x = rim[:2], rim[2:]
     b_val = b_part.astype(jnp.float32)
     x_val = x_part.astype(jnp.float32)
     c_val = c_part.astype(jnp.float32)
@@ -103,18 +113,21 @@
     scale_two = rms_scale(hidden_res)
     scaled_two = hidden_res * scale_two
     normed_ffn = (scaled_two * norm2_scale).astype(jnp.bfloat16)
-    gate_val = product(normed_ffn, whole_gate)
-    up_val = product(normed_ffn, whole_up)
+    grad_out = jnp.where(valid[:, None], cotangent, jnp.zeros_like(cotangent))
+    grad_all = lax.all_gather(grad_out, "fsdp", axis=0, tiled=True)
+    ffn_all = lax.all_gather(normed_ffn, "fsdp", axis=0, tiled=True)
+    both = product(ffn_all, pair)
+    gate_val, up_val = both[:, :part], both[:, part:]
     sigma = jax.nn.sigmoid(gate_val)
     silu_val = gate_val * sigma
     act_val = (silu_val * up_val).astype(jnp.bfloat16)
-    result = hidden_res + product(act_val, whole_down)
-    block_out = jnp.where(valid[:, None], result, 0.0).astype(jnp.bfloat16)
-    grad_out = jnp.where(valid[:, None], cotangent, jnp.zeros_like(cotangent))
-    grad_act = product_right(grad_out, whole_down)
+    grad_act = product_right(grad_all, w_down)
     grad_gate = (grad_act * up_val * sigma * (1.0 + gate_val * (1.0 - sigma))).astype(jnp.bfloat16)
     grad_up = (grad_act * silu_val).astype(jnp.bfloat16)
-    grad_ffn = product_right(grad_gate, whole_gate) + product_right(grad_up, whole_up)
+    grad_pair = jnp.concatenate([grad_gate, grad_up], axis=1)
+    grad_ffn = scattered_sum(product_right(grad_pair, pair))
+    result = hidden_res + scattered_sum(product(act_val, w_down))
+    block_out = jnp.where(valid[:, None], result, 0.0).astype(jnp.bfloat16)
     gain_two = jnp.sum(grad_ffn * scaled_two, axis=0)
     grad_res = grad_out.astype(jnp.float32) + norm_back(
         grad_ffn, scaled_two, scale_two, norm2_scale
@@ -150,26 +163,35 @@
     d_tokens = (grad_res + norm_back(grad_norm_in, scaled_one, scale_one, norm1_scale)).astype(
         jnp.bfloat16
     )
-    d_norm1, d_norm2, d_conv = lax.psum((gain_one, gain_two, conv_grads), ("fsdp", "replica"))
-    grad_pair = jnp.concatenate([grad_gate, grad_up], axis=1)
-    pieces = [
-        product_left(left, right)
-        for left, right in ((normed_in, grad_proj), (y_val, grad_mix), (normed_ffn, grad_pair))
+    small = lax.psum(
+        jnp.concatenate([gain_one[None], gain_two[None], conv_grads], axis=0),
+        ("fsdp", "replica"),
+    )
+    d_norm1, d_norm2, d_conv = small[0], small[1], small[2:]
+    in_part = scattered_sum(product_left(normed_in, grad_proj))
+    out_part = scattered_sum(product_left(y_val, grad_mix))
+    pair_part = product_left(ffn_all, grad_pair).astype(jnp.bfloat16)
+    pair_part = lax.all_to_all(
+        pair_part.reshape(group, own_rows, 2 * part), "fsdp", split_axis=0, concat_axis=0, tiled=True
+    )
+    down_part = product_left(act_val, grad_all)
+    in_part, out_part, pair_part, down_part = [
+        value.astype(jnp.float32)
+        for value in lax.psum(
+            (
+                in_part.astype(jnp.bfloat16),
+                out_part.astype(jnp.bfloat16),
+                pair_part,
+                down_part.astype(jnp.bfloat16),
+            ),
+            "replica",
+        )
     ]
-    rows_part = lax.psum_scatter(
-        jnp.concatenate(pieces, axis=1), "fsdp", scatter_dimension=0, tiled=True
-    )
-    down_part = lax.psum_scatter(
-        product_left(act_val, grad_out), "fsdp", scatter_dimension=0, tiled=True
-    )
-    rows_part, down_part = (
-        lax.psum(rows_part.astype(jnp.bfloat16), "replica").astype(jnp.float32),
-        lax.psum(down_part.astype(jnp.bfloat16), "replica").astype(jnp.float32),
-    )
-    d_w_in = rows_part[:, : 3 * width]
-    d_w_out = rows_part[:, 3 * width : 4 * width]
-    d_w_gate = rows_part[:, 4 * width : 4 * width + hidden]
-    d_w_up = rows_part[:, 4 * width + hidden :]
+    d_w_in = in_part
+    d_w_out = out_part
+    pair_part = pair_part.transpose(1, 0, 2)
+    d_w_gate = pair_part[:, :, :part].reshape(own_rows, hidden)
+    d_w_up = pair_part[:, :, part:].reshape(own_rows, hidden)
     return (
         block_out,
         d_tokens,

time: 2020 us -> 872 us (0.43)
  waiting for transfers between devices: 1810 us -> 650 us
  blocking collectives: 45 us -> 88.6 us
  other arithmetic: 53 us -> 22 us
  matrix products: 87.8 us -> 58.8 us
    reduce_scatter x2 -> x4, waiting for transfers between devices: 1310 us -> 370 us  [scattered_sum(): lax.psum_scatter(value.astype(jnp.bfloat16), 'fsdp', scatter_dimension=0,...]
    all_gather x5 -> x4, waiting for transfers between devices: 495 us -> 246 us  [the longest x1 89.3 us: body(): whole_in = lax.all_gather(w_in, 'fsdp', axis=0, tiled=True)]
    all_to_all x0 -> x1, blocking collectives: none -> 48.4 us  [body(): lax.all_to_all(pair.transpose(1, 0, 2), 'fsdp', split_axis=0, concat_axis...]
    concatenate x1, other arithmetic: 37.3 us -> 0.02 us  [body(): jnp.concatenate(rim_pair, axis=0)]
    all_to_all x0 -> x1, waiting for transfers between devices: none -> 30.9 us  [body(): lax.all_to_all(pair_part.reshape(group, own_rows, 2 * part), 'fsdp', spli...]
  transfers between devices with their start and end apart: 11 -> 12, of which waited for: 8 -> 11; matrix products, arithmetic and copies ran while one was open for 6% -> 8% of each run, Pallas kernels for 0% -> 0%
where the time goes in v1:
time: 872 us; the launch traced here: 871 us
  waiting for transfers between devices  650 us (75%)
  blocking collectives  88.6 us (10%)
  matrix products  58.8 us (7%)
  local copies, waits for them, and re-layouts  25.2 us (3%)
  other arithmetic  22 us (3%)
  between operations  16.8 us (2%)
  starting transfers between devices  9.57 us (1%)
    reduce_scatter x4, waiting for transfers between devices, scattered_sum(): lax.psum_scatter(value.astype(jnp.bfloat16), 'fsdp', scatter_dimension=0,...  370 us
    all_gather x1, waiting for transfers between devices, body(): whole_in = lax.all_gather(w_in, 'fsdp', axis=0, tiled=True)  89.3 us
    all_gather x1, waiting for transfers between devices, body(): grad_all = lax.all_gather(grad_out, 'fsdp', axis=0, tiled=True)  72 us
    all_gather x1, waiting for transfers between devices, body(): whole_out = lax.all_gather(w_out, 'fsdp', axis=0, tiled=True)  55.2 us
    all_to_all x1, blocking collectives, body(): lax.all_to_all(pair.transpose(1, 0, 2), 'fsdp', split_axis=0, concat_axis...  48.4 us
    psum x1, blocking collectives, body(): lax.psum(jnp.concatenate([gain_one[None], gain_two[None], conv_grads], ax...  40.2 us
    all_to_all x1, waiting for transfers between devices, body(): lax.all_to_all(pair_part.reshape(group, own_rows, 2 * part), 'fsdp', spli...  30.9 us
    all_gather x1, waiting for transfers between devices, body(): ffn_all = lax.all_gather(normed_ffn, 'fsdp', axis=0, tiled=True)  29 us
  transfers between devices with their start and end apart: 12, of which 11 were waited for; matrix products, arithmetic and copies ran while one was open for 8% of the time, Pallas kernels for 0%

profile of v1, /device:TPU:0, one launch (start us, length us, event | category | flops | bytes accessed | tf_op | source)
XLA Modules:
  0.0 871.1 jit_solution(7906298135167288233)
XLA Ops:
  7.2 0.7 all-gather.5.cloned.1.call-update
  8.0 0.7 all-gather.7.cloned.1.call-update
  8.7 1.3 add_bitcast_fusion
  11.3 0.8 reduce-window.19
  12.4 0.6 fusion.34
  14.4 0.7 bitcast_subtract_fusion
  15.1 1.1 fusion.25
  16.2 0.7 and_convert_fusion
  16.9 0.7 broadcast_select_fusion.1
  17.5 0.8 fusion.44
  18.4 89.3 %all-gather.5.cloned.1.call-done = bf16[1024,3072]{1,0:T(8,128)(2,1)} async-done(((bf16[64,3072]{1,0:T(8,128)(2,1)}), bf16[1024,3072]{1,0:T(8,128)(2,1)}) %all-gather.5.cloned.1.call-update) | async-done | bytes 6291472 | tf_op jit(solution)/shard_map/all_gather | solution.py:65
  107.7 4.0 convolution_convert_fusion.3
  111.9 1.3 collective-permute-start
  113.2 0.7 collective-permute-done
  114.0 0.3 multiply_add_fusion
  114.3 55.2 %all-gather.7.cloned.1.call-done = bf16[1024,1024]{1,0:T(8,128)(2,1)} async-done(((bf16[64,1024]{1,0:T(8,128)(2,1)}), bf16[1024,1024]{1,0:T(8,128)(2,1)}) %all-gather.7.cloned.1.call-update) | async-done | bytes 2097168 | tf_op jit(solution)/shard_map/all_gather | solution.py:66
  169.5 2.2 multiply_reduce_fusion.3
  171.7 0.8 multiply_convert_fusion.4
  172.6 0.7 iota_compare_fusion
  173.3 1.8 broadcast_select_fusion
  175.1 2.9 reshape.147
  178.0 2.2 copy.36
  180.2 2.9 reshape.148
  183.1 1.3 copy.37
  184.5 1.6 maximum_bitcast_fusion
  186.1 48.4 %all_to_all.10 = bf16[16,64,576]{2,1,0:T(8,128)(2,1)} all-to-all(bf16[16,64,576]{2,1,0:T(8,128)(2,1)S(1)} %maximum_bitcast_fusion), channel_id=1, replica_groups=mesh['fsdp'=16,'replica'=2] {'fsdp'}, dimensions={0} | all-to-all | bytes 2359296 | tf_op jit(solution)/shard_map/all_to_all | solution.py:71
  234.5 29.0 %all-gather.9.cloned.1.call-done = bf16[2176,1024]{1,0:T(8,128)(2,1)} async-done(((bf16[136,1024]{1,0:T(8,128)(2,1)}), bf16[2176,1024]{1,0:T(8,128)(2,1)}) %all-gather.9.cloned.1.call-update) | async-done | bytes 4456464 | tf_op jit(solution)/shard_map/all_gather | solution.py:118
  263.4 7.9 fusion.45
  271.3 72.0 %all-gather.11.cloned.1.call-done = bf16[2176,1024]{1,0:T(8,128)(2,1)} async-done(((bf16[136,1024]{1,0:T(8,128)(2,1)}), bf16[2176,1024]{1,0:T(8,128)(2,1)}) %all-gather.11.cloned.1.call-update) | async-done | bytes 4456464 | tf_op jit(solution)/shard_map/all_gather | solution.py:117
  343.3 7.2 multiply_convert_fusion.1
  350.6 1.0 copy-done.9
  351.6 0.4 copy-done.10
  352.0 5.3 convolution_convert_fusion.1
  357.4 6.0 convolution_convert_fusion.2
  363.5 93.0 %reduce-scatter.7.cloned.1.call-done = bf16[136,1024]{1,0:T(8,128)(2,1)} async-done(((bf16[2176,1024]{1,0:T(8,128)(2,1)}), bf16[136,1024]{1,0:T(8,128)(2,1)}) %reduce-scatter.7.cloned.1.call-update) | async-done | bytes 278544 | tf_op jit(solution)/shard_map/reduce_scatter | solution.py:36
  456.5 1.2 fusion.17
  457.7 101.2 %reduce-scatter.5.cloned.1.call-done = bf16[136,1024]{1,0:T(8,128)(2,1)} async-done(((bf16[2176,1024]{1,0:T(8,128)(2,1)}), bf16[136,1024]{1,0:T(8,128)(2,1)}) %reduce-scatter.5.cloned.1.call-update) | async-done | bytes 278544 | tf_op jit(solution)/shard_map/reduce_scatter | solution.py:36
  558.9 2.1 fusion.13
  561.0 2.1 convolution_convert_fusion.4
  563.2 3.3 multiply_reduce_fusion.1
  566.7 1.6 collective-permute-start.1
  568.6 1.3 collective-permute-done.1
  569.9 0.2 add.126
  570.3 4.6 convolution_convert_fusion
  574.9 6.0 fusion.2
  580.9 1.4 copy.38
  582.3 6.3 all-to-all-start.1
  588.6 5.0 convolution_convert_fusion.5
  593.7 30.9 %all-to-all-done.1 = bf16[16,64,576]{2,1,0:T(8,128)(2,1)S(1)} async-done(((bf16[16,64,576]{2,1,0:T(8,128)(2,1)}), bf16[16,64,576]{2,1,0:T(8,128)(2,1)S(1)}, u32[]{:S(2)}, u32[]{:S(2)}) %all-to-all-start.1) | async-done | bytes 1179680 | tf_op jit(solution)/shard_map/all_to_all | solution.py:174
  624.6 26.4 %reduce-scatter.11.cloned.1.call-done = bf16[64,1024]{1,0:T(8,128)(2,1)} async-done(((bf16[1024,1024]{1,0:T(8,128)(2,1)}), bf16[64,1024]{1,0:T(8,128)(2,1)}) %reduce-scatter.11.cloned.1.call-update) | async-done | bytes 131088 | tf_op jit(solution)/shard_map/reduce_scatter | solution.py:36
  651.0 149.7 %reduce-scatter.9.cloned.1.call-done = bf16[64,3072]{1,0:T(8,128)(2,1)} async-done(((bf16[1024,3072]{1,0:T(8,128)(2,1)}), bf16[64,3072]{1,0:T(8,128)(2,1)}) %reduce-scatter.9.cloned.1.call-update) | async-done | bytes 393232 | tf_op jit(solution)/shard_map/reduce_scatter | solution.py:36
  800.7 5.1 fusion.24
  805.9 40.2 %psum.39 = f32[5,1024]{1,0:T(8,128)S(1)} all-reduce(f32[5,1024]{1,0:T(8,128)S(1)} %concatenate.24), channel_id=1, replica_groups=mesh['fsdp'=16,'replica'=2] {'fsdp','replica'}, use_global_device_ids=true, to_apply=%region_23.24 | all-reduce | flops 5120 | bytes 40960 | tf_op jit(solution)/shard_map/psum | solution.py:166
  846.1 0.6 slice.96
  846.8 0.6 fusion.43
  847.4 0.9 fusion.23
  848.3 1.7 convert_element_type.133
  850.0 1.9 convert_element_type.131
  851.9 2.2 convert_element_type.136
  854.1 0.5 fusion.41
  854.6 2.1 copy.40
  856.7 2.9 reshape.152
  859.6 2.1 copy.39
  861.7 2.9 reshape.151
  (58 shorter events, 1.6 us)
Async XLA Ops:
  7.2 336.2 %copy-start = (bf16[288,1024]{1,0:T(8,128)(2,1)S(1)}, bf16[288,1024]{1,0:T(8,128)(2,1)}, u32[]{:S(2)}) copy-start(bf16[288,1024]{1,0:T(8,128)(2,1)} %param.18) | copy-start | bytes 1769476
  7.2 100.5 %all-gather.5.cloned.1.call-start = ((), (), s32[]{:S(2)}) async-start(), calls=%async_computation.6 | async-start | bytes 6684672 | tf_op jit(solution)/shard_map/all_gather | solution.py:65
  7.9 161.6 %all-gather.7.cloned.1.call-start = ((), (), s32[]{:S(2)}) async-start(), calls=%async_computation.7 | async-start | bytes 2228224 | tf_op jit(solution)/shard_map/all_gather | solution.py:66
  8.7 254.8 %all-gather.9.cloned.1.call-start = ((), (), s32[]{:S(2)}) async-start(), calls=%async_computation.8 | async-start | bytes 4734976 | tf_op jit(solution)/shard_map/all_gather | solution.py:118
  111.7 57.8 %copy-start.2 = (bf16[136,1024]{1,0:T(8,128)(2,1)S(1)}, bf16[136,1024]{1,0:T(8,128)(2,1)}, u32[]{:S(2)}) copy-start(bf16[136,1024]{1,0:T(8,128)(2,1)} %param.12) | copy-start | bytes 835588
  111.9 2.1 collective-permute-start
  113.2 58.5 %copy-start.8 = (f32[1024]{0:T(1024)S(1)}, f32[1024]{0:T(1024)}, u32[]{:S(2)}) copy-start(f32[1024]{0:T(1024)} %param.20) | copy-start | bytes 12292
  172.6 170.8 %all-gather.11.cloned.1.call-start = ((), (), s32[]{:S(2)}) async-start(), calls=%async_computation.10 | async-start | bytes 4734976 | tf_op jit(solution)/shard_map/all_gather | solution.py:117
  175.1 281.4 %reduce-scatter.7.cloned.1.call-start = ((), (), s32[]{:S(2)}) async-start(), calls=%async_computation.11 | async-start | bytes 4734976 | tf_op jit(solution)/shard_map/reduce_scatter | solution.py:36
  343.3 8.7 copy-start.5
  350.6 1.1 copy-start.9
  350.6 1.4 copy-start.10
  357.4 201.5 %reduce-scatter.5.cloned.1.call-start = ((), (), s32[]{:S(2)}) async-start(), calls=%async_computation.9 | async-start | bytes 4734976 | tf_op jit(solution)/shard_map/reduce_scatter | solution.py:36
  363.4 287.6 %reduce-scatter.11.cloned.1.call-start = ((), (), s32[]{:S(2)}) async-start(), calls=%async_computation.13 | async-start | bytes 2228224 | tf_op jit(solution)/shard_map/reduce_scatter | solution.py:36
  563.1 237.6 %reduce-scatter.9.cloned.1.call-start = ((), (), s32[]{:S(2)}) async-start(), calls=%async_computation.12 | async-start | bytes 6684672 | tf_op jit(solution)/shard_map/reduce_scatter | solution.py:36
  566.6 3.6 copy-start.6
  566.7 3.6 copy-start.7
  566.7 3.2 collective-permute-start.1
  582.3 42.3 %all-to-all-start.1 = ((bf16[16,64,576]{2,1,0:T(8,128)(2,1)}), bf16[16,64,576]{2,1,0:T(8,128)(2,1)S(1)}, u32[]{:S(2)}, u32[]{:S(2)}) async-start(bf16[16,64,576]{2,1,0:T(8,128)(2,1)} %bitcast.8), calls=%async_computation.5 | async-start | bytes 2621440 | tf_op jit(solution)/shard_map/all_to_all | solution.py:174
  588.6 259.7 %all-reduce.6.cloned.1.call-start = ((), (), s32[]{:S(2)}) async-start(), calls=%async_computation.14 | async-start | bytes 4849664 | tf_op jit(solution)/shard_map/psum | solution.py:180
  624.6 176.1 %copy-start.4 = (bf16[16,64,576]{2,1,0:T(8,128)(2,1)}, bf16[16,64,576]{2,1,0:T(8,128)(2,1)S(1)}, u32[]{:S(2)}) copy-start(bf16[16,64,576]{2,1,0:T(8,128)(2,1)S(1)} %all-to-all-done.1) | copy-start | bytes 3538948
  848.3 5.9 copy-start.3
  859.6 5.0 copy-start.1
Sparse Core Ops, SparseCore 0:
  10.8 96.8 all-gather.4
  110.5 58.9 all-gather.6
  172.8 90.5 all-gather.8
  266.6 76.6 all-gather.10
  357.5 98.9 reduce-scatter.6
  458.7 100.0 reduce-scatter.4
  563.2 87.7 reduce-scatter.10
  656.3 144.4 reduce-scatter.8
  803.9 21.1 all-reduce.5

commit v2 on v1

--- a/solution.py
+++ b/solution.py
@@ -1,9 +1,229 @@
+import functools
+
 import jax
 import jax.numpy as jnp
 from jax import lax
+from jax.experimental import pallas as pl
+from jax.experimental.pallas import tpu as pltpu
 from jax.sharding import PartitionSpec as P
 
 epsilon = 1e-05
+
+
+class Place:
+    def __init__(self, group):
+        self.me = lax.axis_index("fsdp")
+        self.core = lax.axis_index("replica")
+        self.depth = group // 4
+        self.mask_one = 1 + self.core
+        self.mask_two = 2 - self.core
+        self.bit_one = lax.rem(lax.div(self.me, self.mask_one), 2)
+        self.bit_two = lax.rem(lax.div(self.me, self.mask_two), 2)
+        self.z = lax.div(self.me, 4)
+
+    def index(self, step, flip_one, flip_two):
+        z = lax.rem(self.z + step, self.depth)
+        one = 1 - self.bit_one if flip_one else self.bit_one
+        two = 1 - self.bit_two if flip_two else self.bit_two
+        return 4 * z + self.mask_one * one + self.mask_two * two
+
+    def peers(self):
+        line = [self.index(step, False, False) for step in range(1, self.depth)]
+        return line + [self.index(0, True, False), self.index(0, False, True)]
+
+
+def meet(place, sibling):
+    barrier = pltpu.get_barrier_semaphore()
+    peers = [{"fsdp": peer} for peer in place.peers()]
+    if sibling:
+        peers.append({"replica": 1 - place.core})
+    for peer in peers:
+        pl.semaphore_signal(barrier, inc=1, device_id=peer, device_id_type=pl.DeviceIdType.MESH)
+    pl.semaphore_wait(barrier, len(peers))
+
+
+def push(source, target, send, recv, peer):
+    copy = pltpu.make_async_remote_copy(
+        src_ref=source,
+        dst_ref=target,
+        send_sem=send,
+        recv_sem=recv,
+        device_id=peer,
+        device_id_type=pl.DeviceIdType.MESH,
+    )
+    copy.start()
+    return copy
+
+
+def gather_kernel(group, sibling, x_ref, out_ref, local, sends, recvs):
+    place = Place(group)
+    depth = place.depth
+    meet(place, sibling)
+    half = out_ref.at[place.core] if sibling else out_ref
+    one = {"fsdp": place.index(0, True, False)}
+    two = {"fsdp": place.index(0, False, True)}
+    first, second, shared = [], [], []
+
+    def pass_on(source, number, to_one):
+        row = place.index(-number % depth, not to_one, False)
+        if to_one:
+            at = depth - 1 + number
+            first.append(push(source, half.at[row], sends.at[at], recvs.at[at], one))
+        at = 2 * depth - 1 + len(second)
+        second.append(push(source, half.at[row], sends.at[at], recvs.at[at], two))
+        share(source, row)
+
+    def share(source, row):
+        if sibling:
+            at = 4 * depth - 1 + len(shared)
+            peer = {"replica": 1 - place.core}
+            shared.append(push(source, half.at[row], sends.at[at], recvs.at[at], peer))
+
+    keep = pltpu.make_async_copy(x_ref, half.at[place.me], local)
+    keep.start()
+    line = []
+    for step in range(1, depth):
+        peer = {"fsdp": place.index(step, False, False)}
+        line.append(push(x_ref, half.at[place.me], sends.at[step - 1], recvs.at[step - 1], peer))
+    pass_on(x_ref, 0, True)
+    for step in range(1, depth):
+        line[step - 1].wait_recv()
+        pass_on(half.at[place.index(-step % depth, False, False)], step, True)
+    for number in range(depth):
+        first[number].wait_recv()
+        pass_on(half.at[place.index(-number % depth, True, False)], number, False)
+    for number in range(2 * depth):
+        second[number].wait_recv()
+        row = place.index(-number % depth, number >= depth, True)
+        share(half.at[row], row)
+    for copy in shared:
+        copy.wait_recv()
+    keep.wait()
+    for copy in line + first + second + shared:
+        copy.wait_send()
+
+
+def gathered(block, number, sibling=False):
+    group = lax.axis_size("fsdp")
+    count = group - 1 + (group if sibling else 0)
+    shape = (group,) + block.shape
+    return pl.pallas_call(
+        functools.partial(gather_kernel, group, sibling),
+        out_shape=jax.ShapeDtypeStruct((2,) + shape if sibling else shape, block.dtype),
+        in_specs=[pl.BlockSpec(memory_space=pl.ANY)],
+        out_specs=pl.BlockSpec(memory_space=pl.ANY),
+        scratch_shapes=[
+            pltpu.SemaphoreType.DMA,
+            pltpu.SemaphoreType.DMA((count,)),
+            pltpu.SemaphoreType.DMA((count,)),
+        ],
+        compiler_params=pltpu.CompilerParams(collective_id=number, has_side_effects=True),
+    )(block)
+
+
+def sum_kernel(group, x_ref, out_ref, got_one, got_two, got_line, to_two, to_line, sends, recvs):
+    place = Place(group)
+    depth = place.depth
+    meet(place, False)
+    one = {"fsdp": place.index(0, True, False)}
+    two = {"fsdp": place.index(0, False, True)}
+    wide = jnp.float32
+    first, second, line = [], [], []
+    for flip in (True, False):
+        for step in range(depth):
+            at = len(first)
+            block = x_ref.at[place.index(step + 1, True, flip)]
+            first.append(push(block, got_one.at[at], sends.at[at], recvs.at[at], one))
+    for step in range(depth):
+        first[step].wait_recv()
+        total = x_ref[place.index(step + 1, False, True)].astype(wide) + got_one[step].astype(wide)
+        to_two[step] = total.astype(to_two.dtype)
+        at = 2 * depth + step
+        second.append(push(to_two.at[step], got_two.at[step], sends.at[at], recvs.at[at], two))
+    for step in range(depth):
+        first[depth + step].wait_recv()
+        second[step].wait_recv()
+        total = (
+            x_ref[place.index(step + 1, False, False)].astype(wide)
+            + got_one[depth + step].astype(wide)
+            + got_two[step].astype(wide)
+        )
+        if step < depth - 1:
+            to_line[step] = total.astype(to_line.dtype)
+            at = 3 * depth + step
+            peer = {"fsdp": place.index(step + 1, False, False)}
+            line.append(push(to_line.at[step], got_line.at[step], sends.at[at], recvs.at[at], peer))
+        else:
+            out_ref[...] = total
+    for step in range(depth - 1):
+        line[step].wait_recv()
+        out_ref[...] += got_line[step].astype(wide)
+    for copy in first + second + line:
+        copy.wait_send()
+
+
+def sum_blocks(blocks, number):
+    group = blocks.shape[0]
+    depth = group // 4
+    one = blocks.shape[1:]
+    return pl.pallas_call(
+        functools.partial(sum_kernel, group),
+        out_shape=jax.ShapeDtypeStruct(one, jnp.float32),
+        in_specs=[pl.BlockSpec(memory_space=pltpu.VMEM)],
+        out_specs=pl.BlockSpec(memory_space=pltpu.VMEM),
+        scratch_shapes=[
+            pltpu.VMEM((2 * depth,) + one, blocks.dtype),
+            pltpu.VMEM((depth,) + one, blocks.dtype),
+            pltpu.VMEM((depth - 1,) + one, blocks.dtype),
+            pltpu.VMEM((depth,) + one, blocks.dtype),
+            pltpu.VMEM((depth - 1,) + one, blocks.dtype),
+            pltpu.SemaphoreType.DMA((group - 1,)),
+            pltpu.SemaphoreType.DMA((group - 1,)),
+        ],
+        compiler_params=pltpu.CompilerParams(
+            collective_id=number, has_side_effects=True, vmem_limit_bytes=32 * 1024 * 1024
+        ),
+    )(blocks)
+
+
+def own_kernels():
+    return lax.axis_size("fsdp") == 16 and lax.axis_size("replica") == 2
+
+
+def gather_rows(block, number):
+    if not own_kernels():
+        return lax.all_gather(block, "fsdp", axis=0, tiled=True)
+    return gathered(block, number).reshape(-1, block.shape[1])
+
+
+def other_core(value):
+    return lax.ppermute(value, "replica", [(0, 1), (1, 0)])
+
+
+def cores_sum(value):
+    if lax.axis_size("replica") != 2:
+        return lax.psum(value, "replica").astype(jnp.float32)
+    return value.astype(jnp.float32) + other_core(value).astype(jnp.float32)
+
+
+def mixer_sum(in_grad, out_grad):
+    group = lax.axis_size("fsdp")
+    both = jnp.concatenate([in_grad, out_grad], axis=1).astype(jnp.bfloat16)
+    rows, columns = both.shape
+    if not own_kernels():
+        total = lax.psum_scatter(both, "fsdp", scatter_dimension=0, tiled=True)
+        return cores_sum(total)
+    core = lax.axis_index("replica")
+    left, right = both[:, : columns // 2], both[:, columns // 2 :]
+    mine = jnp.where(core == 0, left, right)
+    theirs = other_core(jnp.where(core == 0, right, left))
+    half = (mine.astype(jnp.float32) + theirs.astype(jnp.float32)).astype(jnp.bfloat16)
+    half = sum_blocks(half.reshape(group, rows // group, columns // 2), 5)
+    half = half.astype(jnp.bfloat16)
+    back = other_core(half)
+    return jnp.concatenate(
+        [jnp.where(core == 0, half, back), jnp.where(core == 0, back, half)], axis=1
+    ).astype(jnp.float32)
 
 
 def passed_along(block, axis, distance):
@@ -32,10 +252,12 @@
     )
 
 
-def scattered_sum(value):
-    return lax.psum_scatter(
-        value.astype(jnp.bfloat16), "fsdp", scatter_dimension=0, tiled=True
-    ).astype(jnp.float32)
+def scattered_sum(value, number):
+    value = value.astype(jnp.bfloat16)
+    if not own_kernels():
+        return lax.psum_scatter(value, "fsdp", scatter_dimension=0, tiled=True).astype(jnp.float32)
+    group = lax.axis_size("fsdp")
+    return sum_blocks(value.reshape(group, value.shape[0] // group, value.shape[1]), number)
 
 
 def norm_back(grad, scaled, scale, gain):
@@ -62,8 +284,15 @@
     hidden = w_gate.shape[1]
     group = lax.axis_size("fsdp")
     part = w_down.shape[0]
-    whole_in = lax.all_gather(w_in, "fsdp", axis=0, tiled=True)
-    whole_out = lax.all_gather(w_out, "fsdp", axis=0, tiled=True)
+    if own_kernels():
+        late = jnp.concatenate([w_in[:, 2 * width :], w_out], axis=1)
+        chosen = jnp.where(lax.axis_index("replica") == 0, w_in[:, : 2 * width], late)
+        halves = gathered(chosen, 0, sibling=True).reshape(2, width, 2 * width)
+        whole_bc, whole_x, whole_out = halves[0], halves[1, :, :width], halves[1, :, width:]
+    else:
+        whole_in = lax.all_gather(w_in, "fsdp", axis=0, tiled=True)
+        whole_bc, whole_x = whole_in[:, : 2 * width], whole_in[:, 2 * width :]
+        whole_out = lax.all_gather(w_out, "fsdp", axis=0, tiled=True)
     own_rows = w_gate.shape[0]
     pair = jnp.concatenate(
         [w_gate.reshape(own_rows, group, part), w_up.reshape(own_rows, group, part)], axis=2
@@ -90,10 +319,10 @@
     scale_one = rms_scale(inputs)
     scaled_one = inputs * scale_one
     normed_in = (scaled_one * norm1_scale).astype(jnp.bfloat16)
-    in_proj = product(normed_in, whole_in).astype(jnp.bfloat16)
-    b_part = in_proj[:, :width]
-    c_part = in_proj[:, width : 2 * width]
-    x_part = in_proj[:, 2 * width :]
+    bc_part = product(normed_in, whole_bc).astype(jnp.bfloat16)
+    b_part = bc_part[:, :width]
+    c_part = bc_part[:, width:]
+    x_part = product(normed_in, whole_x).astype(jnp.bfloat16)
     rim_pair = (
         lax.dynamic_slice_in_dim(b_part, count - 2, 2, 0),
         lax.dynamic_slice_in_dim(x_part, count - 2, 2, 0),
@@ -114,8 +343,8 @@
     scaled_two = hidden_res * scale_two
     normed_ffn = (scaled_two * norm2_scale).astype(jnp.bfloat16)
     grad_out = jnp.where(valid[:, None], cotangent, jnp.zeros_like(cotangent))
-    grad_all = lax.all_gather(grad_out, "fsdp", axis=0, tiled=True)
-    ffn_all = lax.all_gather(normed_ffn, "fsdp", axis=0, tiled=True)
+    grad_all = gather_rows(grad_out, 1)
+    ffn_all = gather_rows(normed_ffn, 2)
     both = product(ffn_all, pair)
     gate_val, up_val = both[:, :part], both[:, part:]
     sigma = jax.nn.sigmoid(gate_val)
@@ -125,8 +354,8 @@
     grad_gate = (grad_act * up_val * sigma * (1.0 + gate_val * (1.0 - sigma))).astype(jnp.bfloat16)
     grad_up = (grad_act * silu_val).astype(jnp.bfloat16)
     grad_pair = jnp.concatenate([grad_gate, grad_up], axis=1)
-    grad_ffn = scattered_sum(product_right(grad_pair, pair))
-    result = hidden_res + scattered_sum(product(act_val, w_down))
+    grad_ffn = scattered_sum(product_right(grad_pair, pair), 3)
+    result = hidden_res + scattered_sum(product(act_val, w_down), 4)
     block_out = jnp.where(valid[:, None], result, 0.0).astype(jnp.bfloat16)
     gain_two = jnp.sum(grad_ffn * scaled_two, axis=0)
     grad_res = grad_out.astype(jnp.float32) + norm_back(
@@ -158,7 +387,9 @@
     grad_proj = jnp.concatenate([grad_u * x_val, grad_c, grad_u * b_val], axis=1).astype(
         jnp.bfloat16
     )
-    grad_norm_in = product_right(grad_proj, whole_in)
+    grad_norm_in = product_right(grad_proj[:, : 2 * width], whole_bc) + product_right(
+        grad_proj[:, 2 * width :], whole_x
+    )
     gain_one = jnp.sum(grad_norm_in * scaled_one, axis=0)
     d_tokens = (grad_res + norm_back(grad_norm_in, scaled_one, scale_one, norm1_scale)).astype(
         jnp.bfloat16
@@ -168,27 +399,16 @@
         ("fsdp", "replica"),
     )
     d_norm1, d_norm2, d_conv = small[0], small[1], small[2:]
-    in_part = scattered_sum(product_left(normed_in, grad_proj))
-    out_part = scattered_sum(product_left(y_val, grad_mix))
+    mix_part = mixer_sum(product_left(normed_in, grad_proj), product_left(y_val, grad_mix))
     pair_part = product_left(ffn_all, grad_pair).astype(jnp.bfloat16)
     pair_part = lax.all_to_all(
         pair_part.reshape(group, own_rows, 2 * part), "fsdp", split_axis=0, concat_axis=0, tiled=True
     )
     down_part = product_left(act_val, grad_all)
-    in_part, out_part, pair_part, down_part = [
-        value.astype(jnp.float32)
-        for value in lax.psum(
-            (
-                in_part.astype(jnp.bfloat16),
-                out_part.astype(jnp.bfloat16),
-                pair_part,
-                down_part.astype(jnp.bfloat16),
-            ),
-            "replica",
-        )
-    ]
-    d_w_in = in_part
-    d_w_out = out_part
+    pair_part = cores_sum(pair_part)
+    down_part = cores_sum(down_part.astype(jnp.bfloat16))
+    d_w_in = mix_part[:, : 3 * width]
+    d_w_out = mix_part[:, 3 * width :]
     pair_part = pair_part.transpose(1, 0, 2)
     d_w_gate = pair_part[:, :, :part].reshape(own_rows, hidden)
     d_w_up = pair_part[:, :, part:].reshape(own_rows, hidden)

time: 872 us -> 538 us (0.62)
  waiting for transfers between devices: 650 us -> 23.9 us
  Pallas kernels: 0 us -> 339 us
  blocking collectives: 88.6 us -> 42.2 us
  starting transfers between devices: 9.57 us -> 22.4 us
  between operations: 16.8 us -> 4.36 us
  matrix products: 58.8 us -> 47.9 us
    reduce_scatter x4 -> x0, waiting for transfers between devices: 370 us -> none  [scattered_sum(): lax.psum_scatter(value.astype(jnp.bfloat16), 'fsdp', scatter_dimension=0,...]
    pallas_call x0 -> x6, Pallas kernels: none -> 339 us  [the longest x3 178 us: gathered(): pl.pallas_call(functools.partial(gather_kernel, group, sibling), out_shap...]
    all_gather x4 -> x0, waiting for transfers between devices: 246 us -> none  [the longest x1 89.3 us: body(): whole_in = lax.all_gather(w_in, 'fsdp', axis=0, tiled=True)]
    all_to_all x1 -> x0, blocking collectives: 48.4 us -> none  [body(): lax.all_to_all(pair.transpose(1, 0, 2), 'fsdp', split_axis=0, concat_axis...]
    dot_general x4 -> x5, matrix products: 20.1 us -> 13.7 us  [product(): return jnp.dot(left, right, preferred_element_type=jnp.float32)]
    dot_general x4 -> x5, matrix products: 21 us -> 21.5 us  [product_right(): lax.dot_general(left, right, (((1,), (1,)), ((), ())), preferred_element_...]
  transfers between devices with their start and end apart: 12 -> 8, of which waited for: 11 -> 2; matrix products, arithmetic and copies ran while one was open for 8% -> 9% of each run, Pallas kernels for 0% -> 34%
where the time goes in v2:
time: 538 us; the launch traced here: 531 us
  Pallas kernels  339 us (63%)
  matrix products  47.9 us (9%)
  blocking collectives  42.2 us (8%)
  local copies, waits for them, and re-layouts  25.9 us (5%)
  other arithmetic  25.6 us (5%)
  waiting for transfers between devices  23.9 us (4%)
  starting transfers between devices  22.4 us (4%)
    pallas_call x3, Pallas kernels, gathered(): pl.pallas_call(functools.partial(gather_kernel, group, sibling), out_shap...  178 us
    pallas_call x3, Pallas kernels, sum_blocks(): pl.pallas_call(functools.partial(sum_kernel, group), out_shape=jax.ShapeD...  161 us
    psum x1, blocking collectives, body(): lax.psum(jnp.concatenate([gain_one[None], gain_two[None], conv_grads], ax...  42.2 us
    all_to_all x1, waiting for transfers between devices, body(): lax.all_to_all(pair_part.reshape(group, own_rows, 2 * part), 'fsdp', spli...  22.4 us
    dot_general x5, matrix products, product_right(): lax.dot_general(left, right, (((1,), (1,)), ((), ())), preferred_element_...  21.5 us
    dot_general x5, matrix products, product(): return jnp.dot(left, right, preferred_element_type=jnp.float32)  13.7 us
    dot_general x4, matrix products, product_left(): lax.dot_general(left, right, (((0,), (0,)), ((), ())), preferred_element_...  12.6 us
  transfers between devices with their start and end apart: 8, of which 2 were waited for; matrix products, arithmetic and copies ran while one was open for 9% of the time, Pallas kernels for 34%

profile of v2, /device:TPU:0, one launch (start us, length us, event | category | flops | bytes accessed | tf_op | source)
XLA Modules:
  0.0 531.3 jit_solution(13469805931371850573)
XLA Ops:
  0.7 2.3 reshape.169
  3.2 1.1 reshape.170
  4.5 1.5 maximum_bitcast_fusion
  6.1 8.4 %all-to-all-start = ((bf16[16,64,576]{2,1,0:T(8,128)(2,1)}), bf16[16,64,576]{2,1,0:T(8,128)(2,1)}, u32[]{:S(2)}, u32[]{:S(2)}) async-start(bf16[16,64,576]{2,1,0:T(8,128)(2,1)} %maximum_bitcast_fusion), calls=%async_computation | async-start | bytes 2621440 | tf_op jit(solution)/shard_map/all_to_all | solution.py:300
  14.6 0.6 add_bitcast_fusion.1
  16.6 0.8 maximum_select_fusion.x_ref
  17.3 72.3 %shard_map.195 = bf16[2,16,64,2048]{3,2,1,0:T(8,128)(2,1)} custom-call(bf16[64,2048]{1,0:T(8,128)(2,1)} %maximum_select_fusion.x_ref), custom_call_target="tpu_custom_call" | custom-call | tf_op jit(solution)/shard_map/pallas_call | solution.py:110
  89.6 2.5 slice.95
  92.2 0.8 convolution_convert_fusion.3
  93.0 1.2 copy-done.3
  94.3 2.2 convert_multiply_fusion.3
  96.5 2.9 collective-permute-start
  99.4 0.2 reduce-window.19
  99.8 0.6 fusion.40
  101.9 0.6 iota_compare_fusion
  102.5 0.7 broadcast_select_fusion.4
  103.2 0.8 broadcast_select_fusion.1.x_ref
  104.0 0.7 and_convert_fusion
  104.7 53.3 %shard_map.198 = bf16[16,136,1024]{2,1,0:T(8,128)(2,1)} custom-call(bf16[136,1024]{1,0:T(8,128)(2,1)} %broadcast_select_fusion.1.x_ref), custom_call_target="tpu_custom_call" | custom-call | tf_op jit(solution)/shard_map/pallas_call | solution.py:110
  158.0 0.3 multiply_add_fusion.1
  158.3 2.4 multiply_reduce_fusion.5
  160.7 0.8 multiply_convert_fusion.4.x_ref
  161.6 52.9 %shard_map.196 = bf16[16,136,1024]{2,1,0:T(8,128)(2,1)} custom-call(bf16[136,1024]{1,0:T(8,128)(2,1)} %multiply_convert_fusion.4.x_ref), custom_call_target="tpu_custom_call" | custom-call | tf_op jit(solution)/shard_map/pallas_call | solution.py:110
  214.4 5.8 %fusion.53 = f32[2176,576]{0,1:T(8,128)S(1)} fusion(bf16[2176,1024]{1,0:T(8,128)(2,1)} %bitcast.76, bf16[1024,576]{1,0:T(8,128)(2,1)} %bitcast.12), kind=kOutput, calls=%fused_computation.119 | convolution fusion | flops 2566914048 | bytes 10649600 | tf_op jit(solution)/shard_map/dot_general | solution.py:240
  220.3 4.8 multiply_convert_fusion.1
  225.1 7.0 %convolution_convert_fusion.1 = bf16[2176,1024]{1,0:T(8,128)(2,1)S(1)} fusion(bf16[1024,576]{1,0:T(8,128)(2,1)} %bitcast.12, bf16[2176,288]{0,1:T(8,128)(2,1)S(1)} %get-tuple-element.21, bf16[2176,288]{0,1:T(8,128)(2,1)S(1)} %get-tuple-element.20), kind=kOutput, calls=%fused_computation.2 | convolution fusion | flops 2574155776 | bytes 8142848 | tf_op jit(solution)/shard_map/dot_general | solution.py:250
  232.1 56.2 %shard_map.199 = f32[136,1024]{1,0:T(8,128)S(1)} custom-call(bf16[16,136,1024]{2,1,0:T(8,128)(2,1)S(1)} %bitcast.64), custom_call_target="tpu_custom_call" | custom-call | tf_op jit(solution)/shard_map/pallas_call | solution.py:169
  288.3 0.3 multiply_reduce_fusion.3
  288.5 2.5 convolution_convert_fusion.2
  291.1 55.9 %shard_map.197 = f32[136,1024]{1,0:T(8,128)S(1)} custom-call(bf16[16,136,1024]{2,1,0:T(8,128)(2,1)S(1)} %bitcast.65), custom_call_target="tpu_custom_call" | custom-call | tf_op jit(solution)/shard_map/pallas_call | solution.py:169
  346.9 1.0 multiply_add_fusion
  347.9 3.9 multiply_reduce_fusion.1
  351.8 1.8 convolution_convert_fusion.4
  353.9 1.3 collective-permute-start.1
  355.4 1.5 collective-permute-done.1
  357.0 1.6 add.122
  358.6 1.3 fusion.22
  359.9 0.7 copy-done.8
  360.6 3.1 convolution_convert_fusion
  363.7 3.0 broadcast_select_fusion
  366.6 1.4 copy-done.2
  368.0 0.9 collective-permute-start.2
  369.0 2.9 fusion.6
  371.9 1.4 copy.42
  373.4 8.9 %all-to-all-start.1 = ((bf16[16,64,576]{2,1,0:T(8,128)(2,1)}), bf16[16,64,576]{2,1,0:T(8,128)(2,1)}, u32[]{:S(2)}, u32[]{:S(2)}) async-start(bf16[16,64,576]{2,1,0:T(8,128)(2,1)} %bitcast.17), calls=%async_computation.1 | async-start | bytes 2621440 | tf_op jit(solution)/shard_map/all_to_all | solution.py:404
  382.3 4.8 convolution_convert_fusion.5
  387.1 2.3 fusion.33
  389.5 22.4 %all-to-all-done.1 = bf16[16,64,576]{2,1,0:T(8,128)(2,1)} async-done(((bf16[16,64,576]{2,1,0:T(8,128)(2,1)}), bf16[16,64,576]{2,1,0:T(8,128)(2,1)}, u32[]{:S(2)}, u32[]{:S(2)}) %all-to-all-start.1) | async-done | bytes 1179680 | tf_op jit(solution)/shard_map/all_to_all | solution.py:404
  411.9 3.5 fusion.30
  415.5 42.2 %psum.7 = f32[5,1024]{1,0:T(8,128)S(1)} all-reduce(f32[5,1024]{1,0:T(8,128)S(1)} %concatenate.41), channel_id=1, replica_groups=mesh['fsdp'=16,'replica'=2] {'fsdp','replica'}, use_global_device_ids=true, to_apply=%region_15.16 | all-reduce | flops 5120 | bytes 40960 | tf_op jit(solution)/shard_map/psum | solution.py:397
  457.7 0.6 slice.139
  458.3 0.6 fusion.51
  459.0 2.0 fusion.29
  460.9 2.6 convert_add_fusion
  463.5 2.2 add_bitcast_fusion
  465.9 4.1 add_convert_fusion
  470.0 48.5 %shard_map.200 = f32[64,2048]{1,0:T(8,128)S(1)} custom-call(bf16[16,64,2048]{2,1,0:T(8,128)(2,1)S(1)} %bitcast.63), custom_call_target="tpu_custom_call" | custom-call | tf_op jit(solution)/shard_map/pallas_call | solution.py:169
  518.7 0.5 fusion.50
  519.2 2.1 copy.44
  521.3 2.9 reshape.178
  524.2 2.1 copy.43
  526.3 3.0 reshape.177
  529.3 0.7 maximum_convert_fusion.1
  530.1 0.9 slice.134
  (115 shorter events, 2.0 us)
Async XLA Ops:
  0.6 219.6 %copy-start = (bf16[288,1024]{1,0:T(8,128)(2,1)S(1)}, bf16[288,1024]{1,0:T(8,128)(2,1)}, u32[]{:S(2)}) copy-start(bf16[288,1024]{1,0:T(8,128)(2,1)} %param.18) | copy-start | bytes 1769476
  0.7 2.5 copy-start.16
  4.5 10.0 %copy-start.7 = (bf16[136,1024]{1,0:T(8,128)(2,1)S(1)}, bf16[136,1024]{1,0:T(8,128)(2,1)}, u32[]{:S(2)}) copy-start(bf16[136,1024]{1,0:T(8,128)(2,1)} %param.12) | copy-start | bytes 835588
  4.5 10.1 %copy-start.27 = (s32[32]{0:T(128)S(1)}, s32[32]{0:T(128)}, u32[]{:S(2)}) copy-start(s32[32]{0:T(128)} %param.22) | copy-start | bytes 388
  4.5 12.1 %copy-start.17 = (bf16[64,3072]{1,0:T(8,128)(2,1)S(1)}, bf16[64,3072]{1,0:T(8,128)(2,1)}, u32[]{:S(2)}) copy-start(bf16[64,3072]{1,0:T(8,128)(2,1)} %param.14) | copy-start | bytes 1179652
  4.5 12.1 %slice-start.4 = ((bf16[64,3072]{1,0:T(8,128)(2,1)}), bf16[64,1024]{1,0:T(8,128)(2,1)S(1)}, s32[]{:S(2)}) async-start(bf16[64,3072]{1,0:T(8,128)(2,1)} %param.14), calls=%async_computation.6 | async-start | bytes 262144 | tf_op jit(solution)/shard_map/slice | solution.py:288
  4.5 12.1 %copy-start.21 = (bf16[64,1024]{1,0:T(8,128)(2,1)S(1)}, bf16[64,1024]{1,0:T(8,128)(2,1)}, u32[]{:S(2)}) copy-start(bf16[64,1024]{1,0:T(8,128)(2,1)} %param.15) | copy-start | bytes 393220
  6.1 208.3 %all-to-all-start = ((bf16[16,64,576]{2,1,0:T(8,128)(2,1)}), bf16[16,64,576]{2,1,0:T(8,128)(2,1)}, u32[]{:S(2)}, u32[]{:S(2)}) async-start(bf16[16,64,576]{2,1,0:T(8,128)(2,1)} %maximum_bitcast_fusion), calls=%async_computation | async-start | bytes 2621440 | tf_op jit(solution)/shard_map/all_to_all | solution.py:300
  89.6 2.5 copy-start.20
  92.1 2.1 copy-start.3
  94.2 5.1 copy-start.28
  94.2 9.0 %copy-start.23 = (f32[3,1024]{1,0:T(4,128)S(1)}, f32[3,1024]{1,0:T(4,128)}, u32[]{:S(2)}) copy-start(f32[3,1024]{1,0:T(4,128)} %param.21) | copy-start | bytes 36868
  94.2 9.0 %copy-start.14 = (bf16[136,1024]{1,0:T(8,128)(2,1)S(1)}, bf16[136,1024]{1,0:T(8,128)(2,1)}, u32[]{:S(2)}) copy-start(bf16[136,1024]{1,0:T(8,128)(2,1)} %param.13) | copy-start | bytes 835588
  96.4 61.5 %copy-start.18 = (bf16[136,1024]{1,0:T(8,128)(2,1)}, bf16[136,1024]{1,0:T(8,128)(2,1)S(1)}, u32[]{:S(2)}) copy-start(bf16[136,1024]{1,0:T(8,128)(2,1)S(1)} %get-tuple-element.43) | copy-start | bytes 835588
  96.5 61.5 %collective-permute-start = (bf16[4,1024]{1,0:T(4,128)(2,1)S(1)}, bf16[4,1024]{1,0:T(4,128)(2,1)S(1)}, u32[]{:S(2)}, u32[]{:S(2)}) collective-permute-start(bf16[4,1024]{1,0:T(4,128)(2,1)S(1)} %pad_maximum_fusion.7), channel_id=1, source_target_pairs={{0,1},{1,2},{2,3},{3,4},{4,5},{5,6},{6,7},{7,8},{8,9},{9,10},{10,1... | collective-permute-start | bytes 24584 | tf_op jit(solution)/shard_map/ppermute | solution.py:232
  158.0 2.7 copy-start.22
  158.3 189.6 %copy-start.11 = (f32[136,1024]{1,0:T(8,128)}, f32[136,1024]{1,0:T(8,128)S(1)}, u32[]{:S(2)}) copy-start(f32[136,1024]{1,0:T(8,128)S(1)} %multiply_add_fusion.1) | copy-start | bytes 1671172
  225.1 7.0 %copy-start.31 = (bf16[2176,288]{0,1:T(8,128)(2,1)}, bf16[2176,288]{0,1:T(8,128)(2,1)S(1)}, u32[]{:S(2)}) copy-start(bf16[2176,288]{0,1:T(8,128)(2,1)S(1)} %get-tuple-element.20) | copy-start | bytes 3760132
  225.1 7.0 %copy-start.33 = (bf16[2176,288]{0,1:T(8,128)(2,1)}, bf16[2176,288]{0,1:T(8,128)(2,1)S(1)}, u32[]{:S(2)}) copy-start(bf16[2176,288]{0,1:T(8,128)(2,1)S(1)} %get-tuple-element.21) | copy-start | bytes 3760132
  225.1 63.5 %copy-start.29 = (bf16[2176,288]{0,1:T(8,128)(2,1)}, bf16[2176,288]{0,1:T(8,128)(2,1)S(1)}, u32[]{:S(2)}) copy-start(bf16[2176,288]{0,1:T(8,128)(2,1)S(1)} %get-tuple-element.22) | copy-start | bytes 3760132
  346.9 1.0 copy-start.19
  353.7 10.0 %copy-start.5 = (bf16[1024,1024]{1,0:T(8,128)(2,1)}, bf16[1024,1024]{1,0:T(8,128)(2,1)S(1)}, u32[]{:S(2)}) copy-start(bf16[1024,1024]{1,0:T(8,128)(2,1)S(1)} %convolution_convert_fusion.4) | copy-start | bytes 6291460
  353.9 3.1 collective-permute-start.1
  355.4 1.5 copy-start.10
  359.8 0.7 copy-start.8
  359.9 3.8 copy-start.12
  360.6 8.4 %slice-start.2 = ((s8[4456448]{0:T(1024)(128)(4,1)}), s8[4194304]{0:T(1024)(128)(4,1)S(1)}, s32[]{:S(2)}) async-start(s8[4456448]{0:T(1024)(128)(4,1)} %bitcast.77), calls=%async_computation.4 | async-start | bytes 8388608
  363.6 4.4 copy-start.2
  363.7 5.3 slice-start.3
  363.7 5.3 copy-start.32
  363.7 5.3 copy-start.34
  368.0 97.7 %collective-permute-start.2 = (bf16[1024,2048]{1,0:T(8,128)(2,1)}, bf16[1024,2048]{1,0:T(8,128)(2,1)}, u32[]{:S(2)}, u32[]{:S(2)}) collective-permute-start(bf16[1024,2048]{1,0:T(8,128)(2,1)} %broadcast_select_fusion), channel_id=1, source_target_pairs={{0,1},{1,0},{2,3},{3,2},{4,5},{5,4},{6,7},{7,6},{8,9},{9,8},{10,11... | collective-permute-start | bytes 12582920 | tf_op jit(solution)/shard_map/ppermute | solution.py:200
  371.9 10.4 %copy-start.30 = (bf16[2176,288]{0,1:T(8,128)(2,1)S(1)}, bf16[2176,288]{0,1:T(8,128)(2,1)}, u32[]{:S(2)}) copy-start(bf16[2176,288]{0,1:T(8,128)(2,1)} %copy-done.29) | copy-start | bytes 3760132
  373.4 38.5 %all-to-all-start.1 = ((bf16[16,64,576]{2,1,0:T(8,128)(2,1)}), bf16[16,64,576]{2,1,0:T(8,128)(2,1)}, u32[]{:S(2)}, u32[]{:S(2)}) async-start(bf16[16,64,576]{2,1,0:T(8,128)(2,1)} %bitcast.17), calls=%async_computation.1 | async-start | bytes 2621440 | tf_op jit(solution)/shard_map/all_to_all | solution.py:404
  382.3 4.8 copy-start.4
  382.3 4.8 copy-start.9
  382.3 4.8 copy-start.15
  387.1 24.8 %copy-start.13 = (bf16[136,1024]{1,0:T(8,128)(2,1)S(1)}, bf16[136,1024]{1,0:T(8,128)(2,1)}, u32[]{:S(2)}) copy-start(bf16[136,1024]{1,0:T(8,128)(2,1)} %copy-done.12) | copy-start | bytes 835588
  387.1 73.8 %collective-permute-start.5 = (bf16[288,1024]{1,0:T(8,128)(2,1)}, bf16[288,1024]{1,0:T(8,128)(2,1)}, u32[]{:S(2)}, u32[]{:S(2)}) collective-permute-start(bf16[288,1024]{1,0:T(8,128)(2,1)} %convolution_convert_fusion.5), channel_id=1, source_target_pairs={{0,1},{1,0},{2,3},{3,2},{4,5},{5,4},{6,7},{7,6},{8,9},{9,8},{10,11... | collective-permute-start | bytes 1769480 | tf_op jit(solution)/shard_map/ppermute | solution.py:200
  389.5 26.0 %copy-start.24 = (f32[1024]{0:T(1024)S(1)}, f32[1024]{0:T(1024)}, u32[]{:S(2)}) copy-start(f32[1024]{0:T(1024)} %get-tuple-element.10) | copy-start | bytes 12292
  389.5 26.0 %copy-start.25 = (f32[1024]{0:T(1024)S(1)}, f32[1024]{0:T(1024)}, u32[]{:S(2)}) copy-start(f32[1024]{0:T(1024)} %get-tuple-element.11) | copy-start | bytes 12292
  389.5 26.0 %copy-start.26 = (f32[1024]{0:T(1024)S(1)}, f32[1024]{0:T(1024)}, u32[]{:S(2)}) copy-start(f32[1024]{0:T(1024)} %get-tuple-element.16) | copy-start | bytes 12292
  411.9 51.6 %collective-permute-start.4 = (bf16[16,64,576]{2,1,0:T(8,128)(2,1)}, bf16[16,64,576]{2,1,0:T(8,128)(2,1)}, u32[]{:S(2)}, u32[]{:S(2)}) collective-permute-start(bf16[16,64,576]{2,1,0:T(8,128)(2,1)} %all-to-all-done.1), channel_id=1, source_target_pairs={{0,1},{1,0},{2,3},{3,2},{4,5},{5,4},{6,7},{7,6},{8,9},{9,8},{10,11... | collective-permute-start | bytes 3538952 | tf_op jit(solution)/shard_map/ppermute | solution.py:200
  411.9 53.8 %slice-start = ((s8[6291456]{0:T(1024)(128)(4,1)}), s8[2097152]{0:T(1024)(128)(4,1)S(1)}, s32[]{:S(2)}) async-start(s8[6291456]{0:T(1024)(128)(4,1)} %bitcast.66), calls=%async_computation.2 | async-start | bytes 4194304
  460.9 4.8 slice-start.1
  463.5 2.4 copy-start.6
  518.6 10.7 %collective-permute-start.3 = (bf16[64,2048]{1,0:T(8,128)(2,1)S(1)}, bf16[64,2048]{1,0:T(8,128)(2,1)S(1)}, u32[]{:S(2)}, u32[]{:S(2)}) collective-permute-start(bf16[64,2048]{1,0:T(8,128)(2,1)S(1)} %convert_element_type.137), channel_id=1, source_target_pairs={{0,1},{1,0},{2,3},{3,2},{4,5},{5,4},{6,7},{7,6},{8,9},{9,8},{10,11... | collective-permute-start | bytes 786440 | tf_op jit(solution)/shard_map/ppermute | solution.py:200
  526.3 4.8 copy-start.1

commit v3 on v2

--- a/solution.py
+++ b/solution.py
@@ -55,135 +55,212 @@
     return copy
 
 
-def gather_kernel(group, sibling, x_ref, out_ref, local, sends, recvs):
+def gather_kernel(group, shares, *refs):
+    count = len(shares)
+    x_refs, outs = refs[:count], refs[count : 2 * count]
+    local, sends, recvs = refs[2 * count :]
     place = Place(group)
     depth = place.depth
-    meet(place, sibling)
-    half = out_ref.at[place.core] if sibling else out_ref
+    meet(place, any(shares))
+    halves = [out.at[place.core] if share else out for out, share in zip(outs, shares)]
     one = {"fsdp": place.index(0, True, False)}
     two = {"fsdp": place.index(0, False, True)}
-    first, second, shared = [], [], []
-
-    def pass_on(source, number, to_one):
+    lanes = range(count)
+    line, first, second, shared = [[[] for _ in lanes] for _ in range(4)]
+
+    def pass_on(lane, source, number, to_one):
+        half = halves[lane]
         row = place.index(-number % depth, not to_one, False)
         if to_one:
             at = depth - 1 + number
-            first.append(push(source, half.at[row], sends.at[at], recvs.at[at], one))
-        at = 2 * depth - 1 + len(second)
-        second.append(push(source, half.at[row], sends.at[at], recvs.at[at], two))
-        share(source, row)
-
-    def share(source, row):
-        if sibling:
-            at = 4 * depth - 1 + len(shared)
+            sems = sends.at[lane, at], recvs.at[lane, at]
+            first[lane].append(push(source, half.at[row], *sems, one))
+        at = 2 * depth - 1 + len(second[lane])
+        sems = sends.at[lane, at], recvs.at[lane, at]
+        second[lane].append(push(source, half.at[row], *sems, two))
+        share(lane, source, row)
+
+    def share(lane, source, row):
+        if shares[lane]:
+            at = 4 * depth - 1 + len(shared[lane])
             peer = {"replica": 1 - place.core}
-            shared.append(push(source, half.at[row], sends.at[at], recvs.at[at], peer))
-
-    keep = pltpu.make_async_copy(x_ref, half.at[place.me], local)
-    keep.start()
-    line = []
+            sems = sends.at[lane, at], recvs.at[lane, at]
+            shared[lane].append(push(source, halves[lane].at[row], *sems, peer))
+
+    keep = []
+    for lane in lanes:
+        own = halves[lane].at[place.me]
+        keep.append(pltpu.make_async_copy(x_refs[lane], own, local.at[lane]))
+        keep[lane].start()
+        for step in range(1, depth):
+            peer = {"fsdp": place.index(step, False, False)}
+            sems = sends.at[lane, step - 1], recvs.at[lane, step - 1]
+            line[lane].append(push(x_refs[lane], own, *sems, peer))
+        pass_on(lane, x_refs[lane], 0, True)
     for step in range(1, depth):
-        peer = {"fsdp": place.index(step, False, False)}
-        line.append(push(x_ref, half.at[place.me], sends.at[step - 1], recvs.at[step - 1], peer))
-    pass_on(x_ref, 0, True)
-    for step in range(1, depth):
-        line[step - 1].wait_recv()
-        pass_on(half.at[place.index(-step % depth, False, False)], step, True)
+        for lane in lanes:
+            line[lane][step - 1].wait_recv()
+            row = place.index(-step % depth, False, False)
+            pass_on(lane, halves[lane].at[row], step, True)
     for number in range(depth):
-        first[number].wait_recv()
-        pass_on(half.at[place.index(-number % depth, True, False)], number, False)
+        for lane in lanes:
+            first[lane][number].wait_recv()
+            row = place.index(-number % depth, True, False)
+            pass_on(lane, halves[lane].at[row], number, False)
     for number in range(2 * depth):
-        second[number].wait_recv()
-        row = place.index(-number % depth, number >= depth, True)
-        share(half.at[row], row)
-    for copy in shared:
-        copy.wait_recv()
-    keep.wait()
-    for copy in line + first + second + shared:
-        copy.wait_send()
-
-
-def gathered(block, number, sibling=False):
+        for lane in lanes:
+            second[lane][number].wait_recv()
+            row = place.index(-number % depth, number >= depth, True)
+            share(lane, halves[lane].at[row], row)
+    for lane in lanes:
+        for copy in shared[lane]:
+            copy.wait_recv()
+        keep[lane].wait()
+        for copy in line[lane] + first[lane] + second[lane] + shared[lane]:
+            copy.wait_send()
+
+
+def gathered(blocks, shares, number):
     group = lax.axis_size("fsdp")
-    count = group - 1 + (group if sibling else 0)
-    shape = (group,) + block.shape
+    count = 2 * group - 1 if any(shares) else group - 1
+    lanes = len(blocks)
+    shapes = [
+        jax.ShapeDtypeStruct(((2,) if share else ()) + (group,) + block.shape, block.dtype)
+        for block, share in zip(blocks, shares)
+    ]
     return pl.pallas_call(
-        functools.partial(gather_kernel, group, sibling),
-        out_shape=jax.ShapeDtypeStruct((2,) + shape if sibling else shape, block.dtype),
-        in_specs=[pl.BlockSpec(memory_space=pl.ANY)],
-        out_specs=pl.BlockSpec(memory_space=pl.ANY),
+        functools.partial(gather_kernel, group, shares),
+        out_shape=shapes,
+        in_specs=[pl.BlockSpec(memory_space=pl.ANY)] * lanes,
+        out_specs=[pl.BlockSpec(memory_space=pl.ANY)] * lanes,
         scratch_shapes=[
-            pltpu.SemaphoreType.DMA,
-            pltpu.SemaphoreType.DMA((count,)),
-            pltpu.SemaphoreType.DMA((count,)),
+            pltpu.SemaphoreType.DMA((lanes,)),
+            pltpu.SemaphoreType.DMA((lanes, count)),
+            pltpu.SemaphoreType.DMA((lanes, count)),
         ],
         compiler_params=pltpu.CompilerParams(collective_id=number, has_side_effects=True),
-    )(block)
-
-
-def sum_kernel(group, x_ref, out_ref, got_one, got_two, got_line, to_two, to_line, sends, recvs):
+        cost_estimate=pl.CostEstimate(flops=0, bytes_accessed=150_000_000, transcendentals=0),
+    )(*blocks)
+
+
+def sum_kernel(group, count, small, *refs):
+    inputs = count + (1 if small else 0)
+    x_refs, outs = refs[:count], refs[inputs : inputs + count]
+    got_one, got_two, got_line, to_two, to_line, sends, recvs = refs[2 * inputs : 2 * inputs + 7]
     place = Place(group)
     depth = place.depth
     meet(place, False)
     one = {"fsdp": place.index(0, True, False)}
     two = {"fsdp": place.index(0, False, True)}
     wide = jnp.float32
-    first, second, line = [], [], []
+    lanes = range(count)
+    first, second, line = [[[] for _ in lanes] for _ in range(3)]
+    little = []
+    if small:
+        little_ref, little_out = refs[count], refs[inputs + count]
+        hold, got, slots, little_sends, little_recvs = refs[2 * inputs + 7 :]
+        sems = [(little_sends.at[i], little_recvs.at[i]) for i in range(depth + 1)]
+        little.append(push(little_ref, got.at[0], *sems[0], one))
     for flip in (True, False):
+        for lane in lanes:
+            for step in range(depth):
+                at = len(first[lane])
+                block = x_refs[lane].at[place.index(step + 1, True, flip)]
+                sem = sends.at[lane, at], recvs.at[lane, at]
+                first[lane].append(push(block, got_one.at[lane, at], *sem, one))
+    if small:
+        little[0].wait_recv()
+        hold[0] = little_ref[...] + got[0]
+        little.append(push(hold.at[0], got.at[1], *sems[1], two))
+    for lane in lanes:
         for step in range(depth):
-            at = len(first)
-            block = x_ref.at[place.index(step + 1, True, flip)]
-            first.append(push(block, got_one.at[at], sends.at[at], recvs.at[at], one))
-    for step in range(depth):
-        first[step].wait_recv()
-        total = x_ref[place.index(step + 1, False, True)].astype(wide) + got_one[step].astype(wide)
-        to_two[step] = total.astype(to_two.dtype)
-        at = 2 * depth + step
-        second.append(push(to_two.at[step], got_two.at[step], sends.at[at], recvs.at[at], two))
-    for step in range(depth):
-        first[depth + step].wait_recv()
-        second[step].wait_recv()
-        total = (
-            x_ref[place.index(step + 1, False, False)].astype(wide)
-            + got_one[depth + step].astype(wide)
-            + got_two[step].astype(wide)
-        )
-        if step < depth - 1:
-            to_line[step] = total.astype(to_line.dtype)
-            at = 3 * depth + step
-            peer = {"fsdp": place.index(step + 1, False, False)}
-            line.append(push(to_line.at[step], got_line.at[step], sends.at[at], recvs.at[at], peer))
-        else:
-            out_ref[...] = total
-    for step in range(depth - 1):
-        line[step].wait_recv()
-        out_ref[...] += got_line[step].astype(wide)
-    for copy in first + second + line:
+            first[lane][step].wait_recv()
+            total = x_refs[lane][place.index(step + 1, False, True)].astype(wide)
+            total = total + got_one[lane, step].astype(wide)
+            to_two[lane, step] = total.astype(to_two.dtype)
+            at = 2 * depth + step
+            sem = sends.at[lane, at], recvs.at[lane, at]
+            second[lane].append(push(to_two.at[lane, step], got_two.at[lane, step], *sem, two))
+    if small:
+        little[1].wait_recv()
+        hold[1] = hold[0] + got[1]
+        slots[place.z] = hold[1]
+        for step in range(1, depth):
+            peer = {"fsdp": place.index(step, False, False)}
+            little.append(push(hold.at[1], slots.at[place.z], *sems[step + 1], peer))
+    for lane in lanes:
+        for step in range(depth):
+            first[lane][depth + step].wait_recv()
+            second[lane][step].wait_recv()
+            total = (
+                x_refs[lane][place.index(step + 1, False, False)].astype(wide)
+                + got_one[lane, depth + step].astype(wide)
+                + got_two[lane, step].astype(wide)
+            )
+            if step < depth - 1:
+                to_line[lane, step] = total.astype(to_line.dtype)
+                at = 3 * depth + step
+                sem = sends.at[lane, at], recvs.at[lane, at]
+                peer = {"fsdp": place.index(step + 1, False, False)}
+                line[lane].append(push(to_line.at[lane, step], got_line.at[lane, step], *sem, peer))
+            else:
+                outs[lane][...] = total
+    for lane in lanes:
+        for step in range(depth - 1):
+            line[lane][step].wait_recv()
+            outs[lane][...] += got_line[lane, step].astype(wide)
+    if small:
+        for copy in little[2:]:
+            copy.wait_recv()
+        total = slots[0]
+        for step in range(1, depth):
+            total = total + slots[step]
+        little_out[...] = total
+    for lane in lanes:
+        for copy in first[lane] + second[lane] + line[lane]:
+            copy.wait_send()
+    for copy in little:
         copy.wait_send()
 
 
-def sum_blocks(blocks, number):
-    group = blocks.shape[0]
+def sum_blocks(arrays, number, little=None):
+    group = arrays[0].shape[0]
     depth = group // 4
-    one = blocks.shape[1:]
+    block = arrays[0].shape[1:]
+    kind = arrays[0].dtype
+    count = len(arrays)
+    shapes = [jax.ShapeDtypeStruct(block, jnp.float32)] * count
+    extra, scratch = [], []
+    if little is not None:
+        extra = [little]
+        shapes = shapes + [jax.ShapeDtypeStruct(little.shape, jnp.float32)]
+        scratch = [
+            pltpu.VMEM((2,) + little.shape, jnp.float32),
+            pltpu.VMEM((2,) + little.shape, jnp.float32),
+            pltpu.VMEM((depth,) + little.shape, jnp.float32),
+            pltpu.SemaphoreType.DMA((depth + 1,)),
+            pltpu.SemaphoreType.DMA((depth + 1,)),
+        ]
     return pl.pallas_call(
-        functools.partial(sum_kernel, group),
-        out_shape=jax.ShapeDtypeStruct(one, jnp.float32),
-        in_specs=[pl.BlockSpec(memory_space=pltpu.VMEM)],
-        out_specs=pl.BlockSpec(memory_space=pltpu.VMEM),
+        functools.partial(sum_kernel, group, count, little is not None),
+        out_shape=shapes,
+        in_specs=[pl.BlockSpec(memory_space=pltpu.VMEM)] * len(shapes),
+        out_specs=[pl.BlockSpec(memory_space=pltpu.VMEM)] * len(shapes),
         scratch_shapes=[
-            pltpu.VMEM((2 * depth,) + one, blocks.dtype),
-            pltpu.VMEM((depth,) + one, blocks.dtype),
-            pltpu.VMEM((depth - 1,) + one, blocks.dtype),
-            pltpu.VMEM((depth,) + one, blocks.dtype),
-            pltpu.VMEM((depth - 1,) + one, blocks.dtype),
-            pltpu.SemaphoreType.DMA((group - 1,)),
-            pltpu.SemaphoreType.DMA((group - 1,)),
-        ],
+            pltpu.VMEM((count, 2 * depth) + block, kind),
+            pltpu.VMEM((count, depth) + block, kind),
+            pltpu.VMEM((count, depth - 1) + block, kind),
+            pltpu.VMEM((count, depth) + block, kind),
+            pltpu.VMEM((count, depth - 1) + block, kind),
+            pltpu.SemaphoreType.DMA((count, group - 1)),
+            pltpu.SemaphoreType.DMA((count, group - 1)),
+        ]
+        + scratch,
         compiler_params=pltpu.CompilerParams(
-            collective_id=number, has_side_effects=True, vmem_limit_bytes=32 * 1024 * 1024
+            collective_id=number, has_side_effects=True, vmem_limit_bytes=36 * 1024 * 1024
         ),
-    )(blocks)
+        cost_estimate=pl.CostEstimate(flops=0, bytes_accessed=150_000_000, transcendentals=0),
+    )(*arrays, *extra)
 
 
 def own_kernels():
@@ -193,7 +270,7 @@
 def gather_rows(block, number):
     if not own_kernels():
         return lax.all_gather(block, "fsdp", axis=0, tiled=True)
-    return gathered(block, number).reshape(-1, block.shape[1])
+    return gathered([block], (False,), number)[0].reshape(-1, block.shape[1])
 
 
 def other_core(value):
@@ -206,24 +283,27 @@
     return value.astype(jnp.float32) + other_core(value).astype(jnp.float32)
 
 
-def mixer_sum(in_grad, out_grad):
+def mixer_sum(in_grad, out_grad, small):
     group = lax.axis_size("fsdp")
     both = jnp.concatenate([in_grad, out_grad], axis=1).astype(jnp.bfloat16)
     rows, columns = both.shape
     if not own_kernels():
         total = lax.psum_scatter(both, "fsdp", scatter_dimension=0, tiled=True)
-        return cores_sum(total)
+        return cores_sum(total), lax.psum(small, ("fsdp", "replica"))
     core = lax.axis_index("replica")
     left, right = both[:, : columns // 2], both[:, columns // 2 :]
     mine = jnp.where(core == 0, left, right)
     theirs = other_core(jnp.where(core == 0, right, left))
     half = (mine.astype(jnp.float32) + theirs.astype(jnp.float32)).astype(jnp.bfloat16)
-    half = sum_blocks(half.reshape(group, rows // group, columns // 2), 5)
+    little = jnp.pad(small, ((0, 8 - small.shape[0]), (0, 0)))
+    half, little = sum_blocks([half.reshape(group, rows // group, columns // 2)], 5, little)
+    little = (little + other_core(little))[: small.shape[0]]
     half = half.astype(jnp.bfloat16)
     back = other_core(half)
-    return jnp.concatenate(
+    whole = jnp.concatenate(
         [jnp.where(core == 0, half, back), jnp.where(core == 0, back, half)], axis=1
-    ).astype(jnp.float32)
+    )
+    return whole.astype(jnp.float32), little
 
 
 def passed_along(block, axis, distance):
@@ -252,12 +332,17 @@
     )
 
 
-def scattered_sum(value, number):
-    value = value.astype(jnp.bfloat16)
+def scattered_sums(values, number):
+    values = [value.astype(jnp.bfloat16) for value in values]
     if not own_kernels():
-        return lax.psum_scatter(value, "fsdp", scatter_dimension=0, tiled=True).astype(jnp.float32)
+        return [
+            lax.psum_scatter(value, "fsdp", scatter_dimension=0, tiled=True).astype(jnp.float32)
+            for value in values
+        ]
     group = lax.axis_size("fsdp")
-    return sum_blocks(value.reshape(group, value.shape[0] // group, value.shape[1]), number)
+    return sum_blocks(
+        [value.reshape(group, value.shape[0] // group, value.shape[1]) for value in values], number
+    )
 
 
 def norm_back(grad, scaled, scale, gain):
@@ -284,15 +369,6 @@
     hidden = w_gate.shape[1]
     group = lax.axis_size("fsdp")
     part = w_down.shape[0]
-    if own_kernels():
-        late = jnp.concatenate([w_in[:, 2 * width :], w_out], axis=1)
-        chosen = jnp.where(lax.axis_index("replica") == 0, w_in[:, : 2 * width], late)
-        halves = gathered(chosen, 0, sibling=True).reshape(2, width, 2 * width)
-        whole_bc, whole_x, whole_out = halves[0], halves[1, :, :width], halves[1, :, width:]
-    else:
-        whole_in = lax.all_gather(w_in, "fsdp", axis=0, tiled=True)
-        whole_bc, whole_x = whole_in[:, : 2 * width], whole_in[:, 2 * width :]
-        whole_out = lax.all_gather(w_out, "fsdp", axis=0, tiled=True)
     own_rows = w_gate.shape[0]
     pair = jnp.concatenate(
         [w_gate.reshape(own_rows, group, part), w_up.reshape(own_rows, group, part)], axis=2
@@ -310,6 +386,19 @@
     row_ids = jnp.arange(rows_dev, dtype=jnp.int32)
     valid = row_ids < count
     position = offset + row_ids
+    grad_out = jnp.where(valid[:, None], cotangent, jnp.zeros_like(cotangent))
+    if own_kernels():
+        late = jnp.concatenate([w_in[:, 2 * width :], w_out], axis=1)
+        chosen = jnp.where(lax.axis_index("replica") == 0, w_in[:, : 2 * width], late)
+        halves, grad_all = gathered([chosen, grad_out], (True, False), 0)
+        halves = halves.reshape(2, width, 2 * width)
+        grad_all = grad_all.reshape(-1, width)
+        whole_bc, whole_x, whole_out = halves[0], halves[1, :, :width], halves[1, :, width:]
+    else:
+        whole_in = lax.all_gather(w_in, "fsdp", axis=0, tiled=True)
+        whole_bc, whole_x = whole_in[:, : 2 * width], whole_in[:, 2 * width :]
+        whole_out = lax.all_gather(w_out, "fsdp", axis=0, tiled=True)
+        grad_all = lax.all_gather(grad_out, "fsdp", axis=0, tiled=True)
     seq_first = jnp.cumsum(seq_lengths) - seq_lengths
     is_start = jnp.any(position[:, None] == seq_first[None, :], axis=1)
     prev_start = jnp.any((position - 1)[:, None] == seq_first[None, :], axis=1)
@@ -342,8 +431,6 @@
     scale_two = rms_scale(hidden_res)
     scaled_two = hidden_res * scale_two
     normed_ffn = (scaled_two * norm2_scale).astype(jnp.bfloat16)
-    grad_out = jnp.where(valid[:, None], cotangent, jnp.zeros_like(cotangent))
-    grad_all = gather_rows(grad_out, 1)
     ffn_all = gather_rows(normed_ffn, 2)
     both = product(ffn_all, pair)
     gate_val, up_val = both[:, :part], both[:, part:]
@@ -354,8 +441,10 @@
     grad_gate = (grad_act * up_val * sigma * (1.0 + gate_val * (1.0 - sigma))).astype(jnp.bfloat16)
     grad_up = (grad_act * silu_val).astype(jnp.bfloat16)
     grad_pair = jnp.concatenate([grad_gate, grad_up], axis=1)
-    grad_ffn = scattered_sum(product_right(grad_pair, pair), 3)
-    result = hidden_res + scattered_sum(product(act_val, w_down), 4)
+    grad_ffn, down_sum = scattered_sums(
+        [product_right(grad_pair, pair), product(act_val, w_down)], 3
+    )
+    result = hidden_res + down_sum
     block_out = jnp.where(valid[:, None], result, 0.0).astype(jnp.bfloat16)
     gain_two = jnp.sum(grad_ffn * scaled_two, axis=0)
     grad_res = grad_out.astype(jnp.float32) + norm_back(
@@ -394,12 +483,12 @@
     d_tokens = (grad_res + norm_back(grad_norm_in, scaled_one, scale_one, norm1_scale)).astype(
         jnp.bfloat16
     )
-    small = lax.psum(
+    mix_part, small = mixer_sum(
+        product_left(normed_in, grad_proj),
+        product_left(y_val, grad_mix),
         jnp.concatenate([gain_one[None], gain_two[None], conv_grads], axis=0),
-        ("fsdp", "replica"),
     )
     d_norm1, d_norm2, d_conv = small[0], small[1], small[2:]
-    mix_part = mixer_sum(product_left(normed_in, grad_proj), product_left(y_val, grad_mix))
     pair_part = product_left(ffn_all, grad_pair).astype(jnp.bfloat16)
     pair_part = lax.all_to_all(
         pair_part.reshape(group, own_rows, 2 * part), "fsdp", split_axis=0, concat_axis=0, tiled=True

time: 538 us -> 487 us (0.905)
  blocking collectives: 42.2 us -> 0 us
  Pallas kernels: 339 us -> 325 us
    psum x1 -> x0, blocking collectives: 42.2 us -> none  [body(): lax.psum(jnp.concatenate([gain_one[None], gain_two[None], conv_grads], ax...]
    pallas_call x6 -> x4, Pallas kernels: 339 us -> 325 us  [the longest x2 171 us: gathered(): pl.pallas_call(functools.partial(gather_kernel, group, shares), out_shape...]
  transfers between devices with their start and end apart: 8 -> 9, of which waited for: 2 -> 2; matrix products, arithmetic and copies ran while one was open for 9% -> 10% of each run, Pallas kernels for 34% -> 36%
where the time goes in v3:
time: 487 us; the launch traced here: 480 us
  Pallas kernels  325 us (67%)
  matrix products  47.5 us (10%)
  waiting for transfers between devices  26.4 us (5%)
  local copies, waits for them, and re-layouts  25.6 us (5%)
  other arithmetic  25.6 us (5%)
  starting transfers between devices  24.6 us (5%)
    pallas_call x2, Pallas kernels, gathered(): pl.pallas_call(functools.partial(gather_kernel, group, shares), out_shape...  171 us
    pallas_call x2, Pallas kernels, sum_blocks(): pl.pallas_call(functools.partial(sum_kernel, group, count, little is not...  154 us
    all_to_all x1, waiting for transfers between devices, body(): lax.all_to_all(pair_part.reshape(group, own_rows, 2 * part), 'fsdp', spli...  24.9 us
    dot_general x5, matrix products, product_right(): lax.dot_general(left, right, (((1,), (1,)), ((), ())), preferred_element_...  21.2 us
    dot_general x5, matrix products, product(): return jnp.dot(left, right, preferred_element_type=jnp.float32)  13.7 us
    dot_general x4, matrix products, product_left(): lax.dot_general(left, right, (((0,), (0,)), ((), ())), preferred_element_...  12.5 us
    all_to_all x1, starting transfers between devices, body(): lax.all_to_all(pair_part.reshape(group, own_rows, 2 * part), 'fsdp', spli...  10.8 us
  transfers between devices with their start and end apart: 9, of which 2 were waited for; matrix products, arithmetic and copies ran while one was open for 10% of the time, Pallas kernels for 36%

profile of v3, /device:TPU:0, one launch (start us, length us, event | category | flops | bytes accessed | tf_op | source)
XLA Modules:
  0.0 479.7 jit_solution(11068572952602479971)
XLA Ops:
  0.7 2.3 reshape.170
  3.0 0.2 copy.39
  3.2 1.1 reshape.171
  4.3 0.2 copy.40
  4.5 1.5 maximum_bitcast_fusion
  6.1 8.5 %all-to-all-start = ((bf16[16,64,576]{2,1,0:T(8,128)(2,1)}), bf16[16,64,576]{2,1,0:T(8,128)(2,1)}, u32[]{:S(2)}, u32[]{:S(2)}) async-start(bf16[16,64,576]{2,1,0:T(8,128)(2,1)} %maximum_bitcast_fusion), calls=%async_computation | async-start | bytes 2621440 | tf_op jit(solution)/shard_map/all_to_all | solution.py:376
  14.7 0.6 add_bitcast_fusion.1
  15.4 0.6 iota_compare_fusion
  17.3 0.8 broadcast_select_fusion.1.refs_1_
  18.1 0.8 maximum_select_fusion.refs_0_
  18.9 111.7 %shard_map.195 = (bf16[2,16,64,2048]{3,2,1,0:T(8,128)(2,1)}, bf16[16,136,1024]{2,1,0:T(8,128)(2,1)}) custom-call(bf16[64,2048]{1,0:T(8,128)(2,1)} %maximum_select_fusion.refs_0_, bf16[136,1024]{1,0:T(8,128)(2,1)} %broadcast_select_fusion.1.refs_1_), custom_call_target="tpu_custom_call" | custom-call | bytes 150000000 | tf_op jit(solution)/shard_map/pallas_call | solution.py:131
  130.7 2.5 slice.99
  133.2 0.8 convolution_convert_fusion.3
  134.0 1.2 copy-done.3
  135.3 2.1 convert_multiply_fusion.3
  137.5 1.5 collective-permute-start
  139.0 0.2 reduce-window.19
  139.5 0.6 fusion.40
  141.5 0.7 broadcast_select_fusion.4
  142.2 0.7 and_convert_fusion
  142.9 0.3 multiply_add_fusion.1
  143.2 2.4 multiply_reduce_fusion.5
  145.6 0.8 multiply_convert_fusion.4.refs_0_
  146.4 59.4 %shard_map.196 = bf16[16,136,1024]{2,1,0:T(8,128)(2,1)} custom-call(bf16[136,1024]{1,0:T(8,128)(2,1)} %multiply_convert_fusion.4.refs_0_), custom_call_target="tpu_custom_call" | custom-call | bytes 150000000 | tf_op jit(solution)/shard_map/pallas_call | solution.py:131
  205.9 5.8 %fusion.53 = f32[2176,576]{0,1:T(8,128)S(1)} fusion(bf16[2176,1024]{1,0:T(8,128)(2,1)} %bitcast.70, bf16[1024,576]{1,0:T(8,128)(2,1)} %bitcast.13), kind=kOutput, calls=%fused_computation.119 | convolution fusion | flops 2566914048 | bytes 10649600 | tf_op jit(solution)/shard_map/dot_general | solution.py:320
  211.7 4.8 multiply_convert_fusion.2
  216.5 2.5 convolution_convert_fusion.2
  219.1 6.0 %convolution_convert_fusion.1 = bf16[2176,1024]{1,0:T(8,128)(2,1)S(1)} fusion(bf16[1024,576]{1,0:T(8,128)(2,1)} %bitcast.13, bf16[2176,288]{0,1:T(8,128)(2,1)S(1)} %get-tuple-element.33, bf16[2176,288]{0,1:T(8,128)(2,1)S(1)} %get-tuple-element.32), kind=kOutput, calls=%fused_computation.2 | convolution fusion | flops 2574155776 | bytes 8142848 | tf_op jit(solution)/shard_map/dot_general | solution.py:330
  225.1 102.4 %shard_map.197 = (f32[136,1024]{1,0:T(8,128)S(1)}, f32[136,1024]{1,0:T(8,128)S(1)}) custom-call(bf16[16,136,1024]{2,1,0:T(8,128)(2,1)S(1)} %bitcast.65, bf16[16,136,1024]{2,1,0:T(8,128)(2,1)S(1)} %bitcast.64), custom_call_target="tpu_custom_call" | custom-call | bytes 150000000 | tf_op jit(solution)/shard_map/pallas_call | solution.py:244
  327.6 0.3 multiply_reduce_fusion.3
  327.8 1.0 multiply_add_fusion
  328.8 3.3 multiply_reduce_fusion.1
  332.1 1.8 convolution_convert_fusion.4
  334.2 1.3 collective-permute-start.1
  335.7 1.5 collective-permute-done.1
  337.3 1.4 add.125
  338.7 1.3 fusion.22
  340.0 0.7 copy-done.7
  340.6 3.1 convolution_convert_fusion
  343.8 3.0 broadcast_select_fusion
  346.7 1.4 copy-done.2
  348.1 1.9 collective-permute-start.2
  350.0 2.9 fusion.6
  352.9 1.4 copy.42
  354.4 10.8 %all-to-all-start.1 = ((bf16[16,64,576]{2,1,0:T(8,128)(2,1)}), bf16[16,64,576]{2,1,0:T(8,128)(2,1)}, u32[]{:S(2)}, u32[]{:S(2)}) async-start(bf16[16,64,576]{2,1,0:T(8,128)(2,1)} %bitcast.22), calls=%async_computation.1 | async-start | bytes 2621440 | tf_op jit(solution)/shard_map/all_to_all | solution.py:493
  365.2 4.7 convolution_convert_fusion.5
  369.9 24.9 %all-to-all-done.1 = bf16[16,64,576]{2,1,0:T(8,128)(2,1)} async-done(((bf16[16,64,576]{2,1,0:T(8,128)(2,1)}), bf16[16,64,576]{2,1,0:T(8,128)(2,1)}, u32[]{:S(2)}, u32[]{:S(2)}) %all-to-all-start.1) | async-done | bytes 1179680 | tf_op jit(solution)/shard_map/all_to_all | solution.py:493
  394.8 3.7 fusion.33
  398.6 3.4 fusion.30
  402.1 2.0 fusion.29
  404.0 2.6 convert_add_fusion
  406.7 2.2 add_bitcast_fusion
  409.0 4.1 add_convert_fusion
  413.2 51.9 %shard_map.198 = (f32[64,2048]{1,0:T(8,128)S(1)}, f32[8,1024]{1,0:T(8,128)S(1)}) custom-call(bf16[16,64,2048]{2,1,0:T(8,128)(2,1)S(1)} %bitcast.63, f32[8,1024]{1,0:T(8,128)S(1)} %pad.19.refs_1_), custom_call_target="tpu_custom_call" | custom-call | bytes 150000000 | tf_op jit(solution)/shard_map/pallas_call | solution.py:244
  465.2 0.6 collective-permute-start.3
  465.7 0.5 fusion.50
  466.3 2.1 copy.44
  468.4 2.9 reshape.178
  471.3 2.1 copy.43
  473.3 2.9 reshape.177
  476.3 0.6 slice.143
  476.9 0.6 fusion.51
  477.5 0.7 maximum_convert_fusion.1
  478.3 0.9 slice.138
  (108 shorter events, 1.6 us)
Async XLA Ops:
  0.6 211.1 %copy-start = (bf16[288,1024]{1,0:T(8,128)(2,1)S(1)}, bf16[288,1024]{1,0:T(8,128)(2,1)}, u32[]{:S(2)}) copy-start(bf16[288,1024]{1,0:T(8,128)(2,1)} %param.18) | copy-start | bytes 1769476
  0.7 2.5 copy-start.15
  4.5 10.1 %copy-start.6 = (bf16[136,1024]{1,0:T(8,128)(2,1)S(1)}, bf16[136,1024]{1,0:T(8,128)(2,1)}, u32[]{:S(2)}) copy-start(bf16[136,1024]{1,0:T(8,128)(2,1)} %param.12) | copy-start | bytes 835588
  4.5 10.2 %copy-start.23 = (s32[32]{0:T(128)S(1)}, s32[32]{0:T(128)}, u32[]{:S(2)}) copy-start(s32[32]{0:T(128)} %param.22) | copy-start | bytes 388
  4.5 12.8 %copy-start.13 = (bf16[136,1024]{1,0:T(8,128)(2,1)S(1)}, bf16[136,1024]{1,0:T(8,128)(2,1)}, u32[]{:S(2)}) copy-start(bf16[136,1024]{1,0:T(8,128)(2,1)} %param.13) | copy-start | bytes 835588
  6.1 12.1 %copy-start.16 = (bf16[64,3072]{1,0:T(8,128)(2,1)S(1)}, bf16[64,3072]{1,0:T(8,128)(2,1)}, u32[]{:S(2)}) copy-start(bf16[64,3072]{1,0:T(8,128)(2,1)} %param.14) | copy-start | bytes 1179652
  6.1 12.1 %slice-start.4 = ((bf16[64,3072]{1,0:T(8,128)(2,1)}), bf16[64,1024]{1,0:T(8,128)(2,1)S(1)}, s32[]{:S(2)}) async-start(bf16[64,3072]{1,0:T(8,128)(2,1)} %param.14), calls=%async_computation.6 | async-start | bytes 262144 | tf_op jit(solution)/shard_map/slice | solution.py:391
  6.1 12.1 %copy-start.20 = (bf16[64,1024]{1,0:T(8,128)(2,1)S(1)}, bf16[64,1024]{1,0:T(8,128)(2,1)}, u32[]{:S(2)}) copy-start(bf16[64,1024]{1,0:T(8,128)(2,1)} %param.15) | copy-start | bytes 393220
  6.1 199.8 %all-to-all-start = ((bf16[16,64,576]{2,1,0:T(8,128)(2,1)}), bf16[16,64,576]{2,1,0:T(8,128)(2,1)}, u32[]{:S(2)}, u32[]{:S(2)}) async-start(bf16[16,64,576]{2,1,0:T(8,128)(2,1)} %maximum_bitcast_fusion), calls=%async_computation | async-start | bytes 2621440 | tf_op jit(solution)/shard_map/all_to_all | solution.py:376
  130.6 2.5 copy-start.19
  133.2 2.1 copy-start.3
  135.2 3.8 copy-start.24
  135.2 6.9 %copy-start.22 = (f32[3,1024]{1,0:T(4,128)S(1)}, f32[3,1024]{1,0:T(4,128)}, u32[]{:S(2)}) copy-start(f32[3,1024]{1,0:T(4,128)} %param.21) | copy-start | bytes 36868
  137.4 5.5 %copy-start.17 = (bf16[136,1024]{1,0:T(8,128)(2,1)}, bf16[136,1024]{1,0:T(8,128)(2,1)S(1)}, u32[]{:S(2)}) copy-start(bf16[136,1024]{1,0:T(8,128)(2,1)S(1)} %get-tuple-element.55) | copy-start | bytes 835588
  137.5 5.4 %collective-permute-start = (bf16[4,1024]{1,0:T(4,128)(2,1)S(1)}, bf16[4,1024]{1,0:T(4,128)(2,1)S(1)}, u32[]{:S(2)}, u32[]{:S(2)}) collective-permute-start(bf16[4,1024]{1,0:T(4,128)(2,1)S(1)} %pad_maximum_fusion.7), channel_id=1, source_target_pairs={{0,1},{1,2},{2,3},{3,4},{4,5},{5,6},{6,7},{7,8},{8,9},{9,10},{10,1... | collective-permute-start | bytes 24584 | tf_op jit(solution)/shard_map/ppermute | solution.py:312
  142.9 2.7 copy-start.21
  143.2 185.6 %copy-start.10 = (f32[136,1024]{1,0:T(8,128)}, f32[136,1024]{1,0:T(8,128)S(1)}, u32[]{:S(2)}) copy-start(f32[136,1024]{1,0:T(8,128)S(1)} %multiply_add_fusion.1) | copy-start | bytes 1671172
  216.5 2.5 copy-start.25
  216.5 2.5 copy-start.27
  216.5 2.5 copy-start.29
  327.6 1.3 copy-start.18
  334.0 9.7 %copy-start.4 = (bf16[1024,1024]{1,0:T(8,128)(2,1)}, bf16[1024,1024]{1,0:T(8,128)(2,1)S(1)}, u32[]{:S(2)}) copy-start(bf16[1024,1024]{1,0:T(8,128)(2,1)S(1)} %convolution_convert_fusion.4) | copy-start | bytes 6291460
  334.2 3.1 collective-permute-start.1
  335.7 1.5 copy-start.9
  339.9 0.7 copy-start.7
  339.9 3.8 copy-start.11
  340.6 9.3 %slice-start.2 = ((s8[4456448]{0:T(1024)(128)(4,1)}), s8[4194304]{0:T(1024)(128)(4,1)S(1)}, s32[]{:S(2)}) async-start(s8[4456448]{0:T(1024)(128)(4,1)} %bitcast.71), calls=%async_computation.4 | async-start | bytes 8388608
  343.7 4.4 copy-start.2
  343.7 6.2 %slice-start.3 = ((s8[4456448]{0:T(1024)(128)(4,1)}), s8[262144]{0:T(1024)(128)(4,1)S(1)}, s32[]{:S(2)}) async-start(s8[4456448]{0:T(1024)(128)(4,1)} %bitcast.71), calls=%async_computation.5 | async-start | bytes 524288
  343.8 6.2 %copy-start.28 = (bf16[2176,288]{0,1:T(8,128)(2,1)S(1)}, bf16[2176,288]{0,1:T(8,128)(2,1)}, u32[]{:S(2)}) copy-start(bf16[2176,288]{0,1:T(8,128)(2,1)} %copy-done.27) | copy-start | bytes 3760132
  343.8 6.2 %copy-start.30 = (bf16[2176,288]{0,1:T(8,128)(2,1)S(1)}, bf16[2176,288]{0,1:T(8,128)(2,1)}, u32[]{:S(2)}) copy-start(bf16[2176,288]{0,1:T(8,128)(2,1)} %copy-done.29) | copy-start | bytes 3760132
  348.1 60.7 %collective-permute-start.2 = (bf16[1024,2048]{1,0:T(8,128)(2,1)}, bf16[1024,2048]{1,0:T(8,128)(2,1)}, u32[]{:S(2)}, u32[]{:S(2)}) collective-permute-start(bf16[1024,2048]{1,0:T(8,128)(2,1)} %broadcast_select_fusion), channel_id=1, source_target_pairs={{0,1},{1,0},{2,3},{3,2},{4,5},{5,4},{6,7},{7,6},{8,9},{9,8},{10,11... | collective-permute-start | bytes 12582920 | tf_op jit(solution)/shard_map/ppermute | solution.py:277
  352.9 12.3 %copy-start.26 = (bf16[2176,288]{0,1:T(8,128)(2,1)S(1)}, bf16[2176,288]{0,1:T(8,128)(2,1)}, u32[]{:S(2)}) copy-start(bf16[2176,288]{0,1:T(8,128)(2,1)} %copy-done.25) | copy-start | bytes 3760132
  354.4 40.4 %all-to-all-start.1 = ((bf16[16,64,576]{2,1,0:T(8,128)(2,1)}), bf16[16,64,576]{2,1,0:T(8,128)(2,1)}, u32[]{:S(2)}, u32[]{:S(2)}) async-start(bf16[16,64,576]{2,1,0:T(8,128)(2,1)} %bitcast.22), calls=%async_computation.1 | async-start | bytes 2621440 | tf_op jit(solution)/shard_map/all_to_all | solution.py:493
  365.2 29.6 %copy-start.8 = (bf16[136,1024]{1,0:T(8,128)(2,1)S(1)}, bf16[136,1024]{1,0:T(8,128)(2,1)}, u32[]{:S(2)}) copy-start(bf16[136,1024]{1,0:T(8,128)(2,1)} %copy-done.7) | copy-start | bytes 835588
  365.2 29.6 %copy-start.14 = (bf16[136,1024]{1,0:T(8,128)(2,1)S(1)}, bf16[136,1024]{1,0:T(8,128)(2,1)}, u32[]{:S(2)}) copy-start(bf16[136,1024]{1,0:T(8,128)(2,1)} %get-tuple-element.42) | copy-start | bytes 835588
  369.9 28.6 %copy-start.12 = (bf16[136,1024]{1,0:T(8,128)(2,1)S(1)}, bf16[136,1024]{1,0:T(8,128)(2,1)}, u32[]{:S(2)}) copy-start(bf16[136,1024]{1,0:T(8,128)(2,1)} %copy-done.11) | copy-start | bytes 835588
  369.9 34.1 %collective-permute-start.5 = (bf16[288,1024]{1,0:T(8,128)(2,1)}, bf16[288,1024]{1,0:T(8,128)(2,1)}, u32[]{:S(2)}, u32[]{:S(2)}) collective-permute-start(bf16[288,1024]{1,0:T(8,128)(2,1)} %convolution_convert_fusion.5), channel_id=1, source_target_pairs={{0,1},{1,0},{2,3},{3,2},{4,5},{5,4},{6,7},{7,6},{8,9},{9,8},{10,11... | collective-permute-start | bytes 1769480 | tf_op jit(solution)/shard_map/ppermute | solution.py:277
  394.8 11.9 %collective-permute-start.4 = (bf16[16,64,576]{2,1,0:T(8,128)(2,1)}, bf16[16,64,576]{2,1,0:T(8,128)(2,1)}, u32[]{:S(2)}, u32[]{:S(2)}) collective-permute-start(bf16[16,64,576]{2,1,0:T(8,128)(2,1)} %all-to-all-done.1), channel_id=1, source_target_pairs={{0,1},{1,0},{2,3},{3,2},{4,5},{5,4},{6,7},{7,6},{8,9},{9,8},{10,11... | collective-permute-start | bytes 3538952 | tf_op jit(solution)/shard_map/ppermute | solution.py:277
  398.5 10.3 %slice-start = ((s8[6291456]{0:T(1024)(128)(4,1)}), s8[2097152]{0:T(1024)(128)(4,1)S(1)}, s32[]{:S(2)}) async-start(s8[6291456]{0:T(1024)(128)(4,1)} %bitcast.66), calls=%async_computation.2 | async-start | bytes 4194304
  404.0 4.8 %slice-start.1 = ((s8[6291456]{0:T(1024)(128)(4,1)}), s8[4194304]{0:T(1024)(128)(4,1)S(1)}, s32[]{:S(2)}) async-start(s8[6291456]{0:T(1024)(128)(4,1)} %bitcast.66), calls=%async_computation.3 | async-start | bytes 8388608
  406.7 2.4 copy-start.5
  465.1 11.2 %collective-permute-start.6 = (f32[8,1024]{1,0:T(8,128)S(1)}, f32[8,1024]{1,0:T(8,128)S(1)}, u32[]{:S(2)}, u32[]{:S(2)}) collective-permute-start(f32[8,1024]{1,0:T(8,128)S(1)} %get-tuple-element.21), channel_id=1, source_target_pairs={{0,1},{1,0},{2,3},{3,2},{4,5},{5,4},{6,7},{7,6},{8,9},{9,8},{10,11... | collective-permute-start | bytes 98312 | tf_op jit(solution)/shard_map/ppermute | solution.py:277
  465.2 12.3 %collective-permute-start.3 = (bf16[64,2048]{1,0:T(8,128)(2,1)S(1)}, bf16[64,2048]{1,0:T(8,128)(2,1)S(1)}, u32[]{:S(2)}, u32[]{:S(2)}) collective-permute-start(bf16[64,2048]{1,0:T(8,128)(2,1)S(1)} %convert_element_type.139), channel_id=1, source_target_pairs={{0,1},{1,0},{2,3},{3,2},{4,5},{5,4},{6,7},{7,6},{8,9},{9,8},{10,11... | collective-permute-start | bytes 786440 | tf_op jit(solution)/shard_map/ppermute | solution.py:277
  476.9 2.4 copy-start.1

commit v4 on v3

--- a/solution.py
+++ b/solution.py
@@ -441,9 +441,15 @@
     grad_gate = (grad_act * up_val * sigma * (1.0 + gate_val * (1.0 - sigma))).astype(jnp.bfloat16)
     grad_up = (grad_act * silu_val).astype(jnp.bfloat16)
     grad_pair = jnp.concatenate([grad_gate, grad_up], axis=1)
+    pair_part = product_left(ffn_all, grad_pair).astype(jnp.bfloat16)
+    pair_part, grad_pair = lax.optimization_barrier((pair_part, grad_pair))
+    pair_part = lax.all_to_all(
+        pair_part.reshape(group, own_rows, 2 * part), "fsdp", split_axis=0, concat_axis=0, tiled=True
+    )
     grad_ffn, down_sum = scattered_sums(
         [product_right(grad_pair, pair), product(act_val, w_down)], 3
     )
+    pair_part, grad_ffn = lax.optimization_barrier((pair_part, grad_ffn))
     result = hidden_res + down_sum
     block_out = jnp.where(valid[:, None], result, 0.0).astype(jnp.bfloat16)
     gain_two = jnp.sum(grad_ffn * scaled_two, axis=0)
@@ -489,10 +495,6 @@
         jnp.concatenate([gain_one[None], gain_two[None], conv_grads], axis=0),
     )
     d_norm1, d_norm2, d_conv = small[0], small[1], small[2:]
-    pair_part = product_left(ffn_all, grad_pair).astype(jnp.bfloat16)
-    pair_part = lax.all_to_all(
-        pair_part.reshape(group, own_rows, 2 * part), "fsdp", split_axis=0, concat_axis=0, tiled=True
-    )
     down_part = product_left(act_val, grad_all)
     pair_part = cores_sum(pair_part)
     down_part = cores_sum(down_part.astype(jnp.bfloat16))

time: 487 us -> 472 us (0.969)
  waiting for transfers between devices: 26.4 us -> 7.61 us
  Pallas kernels: 325 us -> 332 us
  matrix products: 47.5 us -> 41.7 us
    all_to_all x1, waiting for transfers between devices: 24.9 us -> 0.01 us  [body(): lax.all_to_all(pair_part.reshape(group, own_rows, 2 * part), 'fsdp', spli...]
    pallas_call x2, Pallas kernels: 154 us -> 161 us  [sum_blocks(): pl.pallas_call(functools.partial(sum_kernel, group, count, little is not...]
    ppermute x5, waiting for transfers between devices: 0.01 us -> 6.33 us  [other_core(): return lax.ppermute(value, 'replica', [(0, 1), (1, 0)])]
  transfers between devices with their start and end apart: 9 -> 9, of which waited for: 2 -> 2; matrix products, arithmetic and copies ran while one was open for 10% -> 10% of each run, Pallas kernels for 36% -> 60%
where the time goes in v4:
time: 472 us; the launch traced here: 463 us
  Pallas kernels  332 us (70%)
  matrix products  41.7 us (9%)
  local copies, waits for them, and re-layouts  26.8 us (6%)
  other arithmetic  26 us (6%)
  starting transfers between devices  24 us (5%)
  waiting for transfers between devices  7.61 us (2%)
    pallas_call x2, Pallas kernels, gathered(): pl.pallas_call(functools.partial(gather_kernel, group, shares), out_shape...  171 us
    pallas_call x2, Pallas kernels, sum_blocks(): pl.pallas_call(functools.partial(sum_kernel, group, count, little is not...  161 us
    dot_general x5, matrix products, product_right(): lax.dot_general(left, right, (((1,), (1,)), ((), ())), preferred_element_...  18.8 us
    dot_general x5, matrix products, product(): return jnp.dot(left, right, preferred_element_type=jnp.float32)  13.5 us
    all_to_all x1, starting transfers between devices, body(): lax.all_to_all(pair_part.reshape(group, own_rows, 2 * part), 'fsdp', spli...  10.6 us
  transfers between devices with their start and end apart: 9, of which 2 were waited for; matrix products, arithmetic and copies ran while one was open for 10% of the time, Pallas kernels for 60%

profile of v4, /device:TPU:0, one launch (start us, length us, event | category | flops | bytes accessed | tf_op | source)
XLA Modules:
  0.0 462.9 jit_solution(3568944622057338506)
XLA Ops:
  0.7 2.3 reshape.170
  3.2 1.1 reshape.171
  4.5 1.5 maximum_bitcast_fusion
  6.1 8.5 %all-to-all-start = ((bf16[16,64,576]{2,1,0:T(8,128)(2,1)}), bf16[16,64,576]{2,1,0:T(8,128)(2,1)}, u32[]{:S(2)}, u32[]{:S(2)}) async-start(bf16[16,64,576]{2,1,0:T(8,128)(2,1)} %maximum_bitcast_fusion), calls=%async_computation | async-start | bytes 2621440 | tf_op jit(solution)/shard_map/all_to_all | solution.py:376
  14.7 0.6 add_bitcast_fusion.1
  15.4 0.6 iota_compare_fusion
  17.3 0.8 broadcast_select_fusion.1.refs_1_
  18.1 0.8 maximum_select_fusion.refs_0_
  18.9 111.7 %shard_map.195 = (bf16[2,16,64,2048]{3,2,1,0:T(8,128)(2,1)}, bf16[16,136,1024]{2,1,0:T(8,128)(2,1)}) custom-call(bf16[64,2048]{1,0:T(8,128)(2,1)} %maximum_select_fusion.refs_0_, bf16[136,1024]{1,0:T(8,128)(2,1)} %broadcast_select_fusion.1.refs_1_), custom_call_target="tpu_custom_call" | custom-call | bytes 150000000 | tf_op jit(solution)/shard_map/pallas_call | solution.py:131
  130.7 2.5 slice.99
  133.2 0.8 convolution_convert_fusion.3
  134.0 1.1 copy-done.3
  135.2 2.1 convert_multiply_fusion.3
  137.4 1.5 collective-permute-start
  139.4 0.6 fusion.38
  141.5 0.7 broadcast_select_fusion.4
  142.1 0.7 and_convert_fusion
  142.9 0.3 multiply_add_fusion.1
  143.2 2.4 multiply_reduce_fusion.5
  145.6 0.8 multiply_convert_fusion.4.refs_0_
  146.4 59.4 %shard_map.196 = bf16[16,136,1024]{2,1,0:T(8,128)(2,1)} custom-call(bf16[136,1024]{1,0:T(8,128)(2,1)} %multiply_convert_fusion.4.refs_0_), custom_call_target="tpu_custom_call" | custom-call | bytes 150000000 | tf_op jit(solution)/shard_map/pallas_call | solution.py:131
  205.9 5.7 %fusion.49 = f32[2176,576]{0,1:T(8,128)S(1)} fusion(bf16[2176,1024]{1,0:T(8,128)(2,1)} %bitcast.69, bf16[1024,576]{1,0:T(8,128)(2,1)} %bitcast.13), kind=kOutput, calls=%fused_computation.116 | convolution fusion | flops 2566914048 | bytes 10649600 | tf_op jit(solution)/shard_map/dot_general | solution.py:320
  211.6 5.8 %multiply_convert_fusion.2 = (bf16[2176,288]{0,1:T(8,128)(2,1)S(1)}, bf16[2176,288]{0,1:T(8,128)(2,1)S(1)}, bf16[2176,288]{0,1:T(8,128)(2,1)}) fusion(f32[2176,576]{0,1:T(8,128)S(1)} %fusion.49, bf16[2176,1024]{1,0:T(8,128)(2,1)} %bitcast.90, bf16[288,1024]{1,0:T(8,128)(2,1)S(1)} %copy-done), kind=kOutput, calls=%fused_computation.10 | convolution fusion | flops 1292857344 | bytes 13819904 | tf_op jit(solution)/shard_map/dot_general | solution.py:330
  217.4 4.0 convolution_convert_fusion.5
  221.3 1.7 pad_maximum_fusion.1
  223.0 2.5 copy.41
  225.5 10.6 %all-to-all-start.1 = ((bf16[16,64,576]{2,1,0:T(8,128)(2,1)}), bf16[16,64,576]{2,1,0:T(8,128)(2,1)}, u32[]{:S(2)}, u32[]{:S(2)}) async-start(bf16[16,64,576]{2,1,0:T(8,128)(2,1)} %bitcast.16), calls=%async_computation.1 | async-start | bytes 2621440 | tf_op jit(solution)/shard_map/all_to_all | solution.py:446
  236.2 2.5 convolution_convert_fusion.2
  238.7 5.5 %convolution_convert_fusion.1 = bf16[2176,1024]{1,0:T(8,128)(2,1)S(1)} fusion(bf16[2176,576]{0,1:T(8,128)(2,1)S(1)} %copy-done.6, bf16[1024,576]{1,0:T(8,128)(2,1)} %bitcast.13), kind=kOutput, calls=%fused_computation.2 | convolution fusion | flops 2569142272 | bytes 8142848 | tf_op jit(solution)/shard_map/dot_general | solution.py:330
  244.2 105.7 %shard_map.197 = (f32[136,1024]{1,0:T(8,128)S(1)}, f32[136,1024]{1,0:T(8,128)S(1)}) custom-call(bf16[16,136,1024]{2,1,0:T(8,128)(2,1)S(1)} %bitcast.66, bf16[16,136,1024]{2,1,0:T(8,128)(2,1)S(1)} %bitcast.65), custom_call_target="tpu_custom_call" | custom-call | bytes 150000000 | tf_op jit(solution)/shard_map/pallas_call | solution.py:244
  350.0 0.3 multiply_reduce_fusion.3
  350.3 1.0 multiply_add_fusion
  351.3 3.3 multiply_reduce_fusion.1
  354.6 0.8 convolution_convert_fusion.4
  355.6 1.5 collective-permute-start.1
  357.4 1.3 collective-permute-done.1
  358.7 1.4 add.125
  360.1 1.3 fusion.20
  361.4 3.1 convolution_convert_fusion
  364.5 2.9 broadcast_select_fusion
  367.4 1.0 copy-done.2
  368.4 0.6 collective-permute-start.2
  369.1 1.5 convolution_convert_fusion.6
  370.7 0.5 collective-permute-start.4
  371.2 6.3 %collective-permute-done.5 = bf16[288,1024]{1,0:T(8,128)(2,1)S(1)} collective-permute-done((bf16[288,1024]{1,0:T(8,128)(2,1)S(1)}, bf16[288,1024]{1,0:T(8,128)(2,1)S(1)}, u32[]{:S(2)}, u32[]{:S(2)}) %collective-permute-start.5) | collective-permute-done | bytes 589856 | tf_op jit(solution)/shard_map/ppermute | solution.py:277
  377.5 1.2 convert_add_fusion
  378.8 1.5 fusion.31
  380.3 2.6 fusion.28
  382.9 0.7 concatenate.40
  383.6 0.8 pad.19.refs_1_
  384.3 0.9 fusion.27
  385.2 2.0 add_bitcast_fusion
  387.3 5.4 %add_convert_fusion = bf16[1024,2048]{1,0:T(8,128)(2,1)S(1)} fusion(bf16[1024,2048]{1,0:T(8,128)(2,1)} %collective-permute-done.2, pred[]{:T(512)S(6)} %eq.18, bf16[1024,3072]{1,0:T(8,128)(2,1)} %copy-done.2, bf16[1024,1024]{1,0:T(8,128)(2,1)S(1)} %convolution_convert_fusion.4), kind=kLoop, calls=%fused_computation | loop fusion | flops 18874368 | bytes 20971520 | tf_op jit(solution)/shard_map/convert_element_type | solution.py:297
  392.7 55.5 %shard_map.198 = (f32[64,2048]{1,0:T(8,128)S(1)}, f32[8,1024]{1,0:T(8,128)S(1)}) custom-call(bf16[16,64,2048]{2,1,0:T(8,128)(2,1)S(1)} %bitcast.64, f32[8,1024]{1,0:T(8,128)S(1)} %pad.19.refs_1_), custom_call_target="tpu_custom_call" | custom-call | bytes 150000000 | tf_op jit(solution)/shard_map/pallas_call | solution.py:244
  448.3 0.6 collective-permute-start.3
  448.9 0.5 fusion.46
  449.4 2.1 copy.44
  451.5 2.9 reshape.178
  454.4 2.1 copy.43
  456.5 2.9 reshape.177
  459.4 0.6 slice.143
  460.0 0.6 fusion.47
  460.7 0.7 maximum_convert_fusion.1
  461.5 0.9 slice.138
  (107 shorter events, 2.0 us)
Async XLA Ops:
  0.6 210.9 %copy-start = (bf16[288,1024]{1,0:T(8,128)(2,1)S(1)}, bf16[288,1024]{1,0:T(8,128)(2,1)}, u32[]{:S(2)}) copy-start(bf16[288,1024]{1,0:T(8,128)(2,1)} %param.18) | copy-start | bytes 1769476
  0.7 2.5 copy-start.12
  4.5 10.1 %copy-start.5 = (bf16[136,1024]{1,0:T(8,128)(2,1)S(1)}, bf16[136,1024]{1,0:T(8,128)(2,1)}, u32[]{:S(2)}) copy-start(bf16[136,1024]{1,0:T(8,128)(2,1)} %param.12) | copy-start | bytes 835588
  4.5 10.2 %copy-start.26 = (s32[32]{0:T(128)S(1)}, s32[32]{0:T(128)}, u32[]{:S(2)}) copy-start(s32[32]{0:T(128)} %param.22) | copy-start | bytes 388
  4.5 12.8 %copy-start.10 = (bf16[136,1024]{1,0:T(8,128)(2,1)S(1)}, bf16[136,1024]{1,0:T(8,128)(2,1)}, u32[]{:S(2)}) copy-start(bf16[136,1024]{1,0:T(8,128)(2,1)} %param.13) | copy-start | bytes 835588
  6.1 12.1 %copy-start.15 = (bf16[64,3072]{1,0:T(8,128)(2,1)S(1)}, bf16[64,3072]{1,0:T(8,128)(2,1)}, u32[]{:S(2)}) copy-start(bf16[64,3072]{1,0:T(8,128)(2,1)} %param.14) | copy-start | bytes 1179652
  6.1 12.1 %slice-start.2 = ((bf16[64,3072]{1,0:T(8,128)(2,1)}), bf16[64,1024]{1,0:T(8,128)(2,1)S(1)}, s32[]{:S(2)}) async-start(bf16[64,3072]{1,0:T(8,128)(2,1)} %param.14), calls=%async_computation.4 | async-start | bytes 262144 | tf_op jit(solution)/shard_map/slice | solution.py:391
  6.1 12.1 %copy-start.19 = (bf16[64,1024]{1,0:T(8,128)(2,1)S(1)}, bf16[64,1024]{1,0:T(8,128)(2,1)}, u32[]{:S(2)}) copy-start(bf16[64,1024]{1,0:T(8,128)(2,1)} %param.15) | copy-start | bytes 393220
  6.1 199.8 %all-to-all-start = ((bf16[16,64,576]{2,1,0:T(8,128)(2,1)}), bf16[16,64,576]{2,1,0:T(8,128)(2,1)}, u32[]{:S(2)}, u32[]{:S(2)}) async-start(bf16[16,64,576]{2,1,0:T(8,128)(2,1)} %maximum_bitcast_fusion), calls=%async_computation | async-start | bytes 2621440 | tf_op jit(solution)/shard_map/all_to_all | solution.py:376
  16.0 117.1 %copy-start.24 = (pred[136]{0:T(512)(128)(4,1)}, pred[136]{0:T(512)(128)(4,1)S(1)}, u32[]{:S(2)}) copy-start(pred[136]{0:T(512)(128)(4,1)S(1)} %iota_compare_fusion) | copy-start | bytes 412
  130.6 2.5 copy-start.18
  133.2 2.0 copy-start.3
  135.2 3.8 copy-start.27
  135.2 6.9 %copy-start.23 = (f32[3,1024]{1,0:T(4,128)S(1)}, f32[3,1024]{1,0:T(4,128)}, u32[]{:S(2)}) copy-start(f32[3,1024]{1,0:T(4,128)} %param.21) | copy-start | bytes 36868
  137.3 5.5 %copy-start.16 = (bf16[136,1024]{1,0:T(8,128)(2,1)}, bf16[136,1024]{1,0:T(8,128)(2,1)S(1)}, u32[]{:S(2)}) copy-start(bf16[136,1024]{1,0:T(8,128)(2,1)S(1)} %get-tuple-element.63) | copy-start | bytes 835588
  137.4 5.5 %copy-start.13 = (f32[136,1024]{1,0:T(8,128)}, f32[136,1024]{1,0:T(8,128)S(1)}, u32[]{:S(2)}) copy-start(f32[136,1024]{1,0:T(8,128)S(1)} %get-tuple-element.62) | copy-start | bytes 1671172
  137.4 5.4 %collective-permute-start = (bf16[4,1024]{1,0:T(4,128)(2,1)S(1)}, bf16[4,1024]{1,0:T(4,128)(2,1)S(1)}, u32[]{:S(2)}, u32[]{:S(2)}) collective-permute-start(bf16[4,1024]{1,0:T(4,128)(2,1)S(1)} %pad_maximum_fusion.3), channel_id=1, source_target_pairs={{0,1},{1,2},{2,3},{3,4},{4,5},{5,6},{6,7},{7,8},{8,9},{9,10},{10,1... | collective-permute-start | bytes 24584 | tf_op jit(solution)/shard_map/ppermute | solution.py:312
  142.8 2.8 copy-start.21
  142.9 2.7 copy-start.20
  143.2 62.7 %copy-start.8 = (f32[136,1024]{1,0:T(8,128)}, f32[136,1024]{1,0:T(8,128)S(1)}, u32[]{:S(2)}) copy-start(f32[136,1024]{1,0:T(8,128)S(1)} %multiply_add_fusion.1) | copy-start | bytes 1671172
  205.9 11.5 %slice-start = ((s8[4456448]{0:T(1024)(128)(4,1)}), s8[262144]{0:T(1024)(128)(4,1)S(1)}, s32[]{:S(2)}) async-start(s8[4456448]{0:T(1024)(128)(4,1)} %bitcast.70), calls=%async_computation.2 | async-start | bytes 524288
  211.6 5.8 %slice-start.1 = ((s8[4456448]{0:T(1024)(128)(4,1)}), s8[4194304]{0:T(1024)(128)(4,1)S(1)}, s32[]{:S(2)}) async-start(s8[4456448]{0:T(1024)(128)(4,1)} %bitcast.70), calls=%async_computation.3 | async-start | bytes 8388608
  223.0 13.1 %copy-start.28 = (bf16[2176,288]{0,1:T(8,128)(2,1)S(1)}, bf16[2176,288]{0,1:T(8,128)(2,1)}, u32[]{:S(2)}) copy-start(bf16[2176,288]{0,1:T(8,128)(2,1)} %get-tuple-element.42) | copy-start | bytes 3760132
  225.5 124.4 %all-to-all-start.1 = ((bf16[16,64,576]{2,1,0:T(8,128)(2,1)}), bf16[16,64,576]{2,1,0:T(8,128)(2,1)}, u32[]{:S(2)}, u32[]{:S(2)}) async-start(bf16[16,64,576]{2,1,0:T(8,128)(2,1)} %bitcast.16), calls=%async_computation.1 | async-start | bytes 2621440 | tf_op jit(solution)/shard_map/all_to_all | solution.py:446
  236.2 2.5 copy-start.6
  244.2 106.1 %copy-start.25 = (pred[136]{0:T(512)(128)(4,1)S(1)}, pred[136]{0:T(512)(128)(4,1)}, u32[]{:S(2)}) copy-start(pred[136]{0:T(512)(128)(4,1)} %copy-done.24) | copy-start | bytes 412
  349.9 1.3 copy-start.22
  350.0 1.3 copy-start.9
  350.0 1.3 copy-start.14
  350.0 1.3 copy-start.17
  355.6 3.1 collective-permute-start.1
  357.4 1.3 copy-start.7
  361.4 7.7 %slice-start.3 = ((s8[4456448]{0:T(1024)(128)(4,1)}), s8[4194304]{0:T(1024)(128)(4,1)S(1)}, s32[]{:S(2)}) async-start(s8[4456448]{0:T(1024)(128)(4,1)} %bitcast.91), calls=%async_computation.5 | async-start | bytes 8388608
  364.5 4.0 copy-start.2
  364.5 4.6 slice-start.4
  364.5 4.6 copy-start.29
  368.4 18.8 %collective-permute-start.2 = (bf16[1024,2048]{1,0:T(8,128)(2,1)}, bf16[1024,2048]{1,0:T(8,128)(2,1)}, u32[]{:S(2)}, u32[]{:S(2)}) collective-permute-start(bf16[1024,2048]{1,0:T(8,128)(2,1)} %broadcast_select_fusion), channel_id=1, source_target_pairs={{0,1},{1,0},{2,3},{3,2},{4,5},{5,4},{6,7},{7,6},{8,9},{9,8},{10,11... | collective-permute-start | bytes 12582920 | tf_op jit(solution)/shard_map/ppermute | solution.py:277
  369.1 9.7 %copy-start.4 = (bf16[1,16,64,2048]{3,2,1,0:T(8,128)(2,1)S(1)}, bf16[1,16,64,2048]{3,2,1,0:T(8,128)(2,1)}, u32[]{:S(2)}) copy-start(bf16[1,16,64,2048]{3,2,1,0:T(8,128)(2,1)} %copy-done.3) | copy-start | bytes 12582916
  370.6 8.1 %copy-start.11 = (bf16[136,1024]{1,0:T(8,128)(2,1)S(1)}, bf16[136,1024]{1,0:T(8,128)(2,1)}, u32[]{:S(2)}) copy-start(bf16[136,1024]{1,0:T(8,128)(2,1)} %get-tuple-element.50) | copy-start | bytes 835588
  370.7 6.9 %collective-permute-start.5 = (bf16[288,1024]{1,0:T(8,128)(2,1)S(1)}, bf16[288,1024]{1,0:T(8,128)(2,1)S(1)}, u32[]{:S(2)}, u32[]{:S(2)}) collective-permute-start(bf16[288,1024]{1,0:T(8,128)(2,1)S(1)} %convolution_convert_fusion.6), channel_id=1, source_target_pairs={{0,1},{1,0},{2,3},{3,2},{4,5},{5,4},{6,7},{7,6},{8,9},{9,8},{10,11... | collective-permute-start | bytes 1769480 | tf_op jit(solution)/shard_map/ppermute | solution.py:277
  370.7 14.5 %collective-permute-start.4 = (bf16[16,64,576]{2,1,0:T(8,128)(2,1)}, bf16[16,64,576]{2,1,0:T(8,128)(2,1)}, u32[]{:S(2)}, u32[]{:S(2)}) collective-permute-start(bf16[16,64,576]{2,1,0:T(8,128)(2,1)} %all-to-all-done.1), channel_id=1, source_target_pairs={{0,1},{1,0},{2,3},{3,2},{4,5},{5,4},{6,7},{7,6},{8,9},{9,8},{10,11... | collective-permute-start | bytes 3538952 | tf_op jit(solution)/shard_map/ppermute | solution.py:277
  448.2 11.2 %collective-permute-start.6 = (f32[8,1024]{1,0:T(8,128)S(1)}, f32[8,1024]{1,0:T(8,128)S(1)}, u32[]{:S(2)}, u32[]{:S(2)}) collective-permute-start(f32[8,1024]{1,0:T(8,128)S(1)} %get-tuple-element.29), channel_id=1, source_target_pairs={{0,1},{1,0},{2,3},{3,2},{4,5},{5,4},{6,7},{7,6},{8,9},{9,8},{10,11... | collective-permute-start | bytes 98312 | tf_op jit(solution)/shard_map/ppermute | solution.py:277
  448.3 12.3 %collective-permute-start.3 = (bf16[64,2048]{1,0:T(8,128)(2,1)S(1)}, bf16[64,2048]{1,0:T(8,128)(2,1)S(1)}, u32[]{:S(2)}, u32[]{:S(2)}) collective-permute-start(bf16[64,2048]{1,0:T(8,128)(2,1)S(1)} %convert_element_type.140), channel_id=1, source_target_pairs={{0,1},{1,0},{2,3},{3,2},{4,5},{5,4},{6,7},{7,6},{8,9},{9,8},{10,11... | collective-permute-start | bytes 786440 | tf_op jit(solution)/shard_map/ppermute | solution.py:277
  460.0 2.4 copy-start.1
